TPU v7x, 32 devices: a whole 2x2x4 slice. The times are simulated.
32 devices in a mesh: dp: 8 (over z, x), mp: 4 (over y, core).
Axes of the slice: x: 2, y: 2, z: 4, core: 2. Of those that a mesh axis runs over, the one named last changes fastest.
Arguments:
- tokens: bfloat16 [8192, 768], P('dp'), may hold values from -6 to 6
- routes: int32 [8192, 1], P('dp'), may hold values from 0 to 7
- lengths: int32 [4], replicated, may hold values from 512 to 2048, as said below
- cotangent: bfloat16 [8192, 768], P('dp'), may hold values from -6 to 6
- first_gain: bfloat16 [768], replicated, may hold values from 0.5 to 1.5
- mixer_in: bfloat16 [768, 2, 1536], P(None, None, 'mp'), may hold values from -0.21875 to 0.21875
- conv_weight: bfloat16 [4, 1536], P(None, 'mp'), may hold values from -3 to 3
- conv_bias: bfloat16 [1536], P('mp'), may hold values from -1.5 to 1.5
- select_weight: bfloat16 [1536, 80], P('mp'), may hold values from -0.15625 to 0.15625
- step_weight: bfloat16 [48, 1536], P(None, 'mp'), may hold values from -0.875 to 0.875
- step_bias: bfloat16 [1536], P('mp'), may hold values from -4.5 to -1.5
- decay_log: bfloat16 [16, 1536], P(None, 'mp'), may hold values from -7 to 2
- skip_gain: bfloat16 [1536], P('mp'), may hold values from 0.5 to 1.5
- mixer_out: bfloat16 [1536, 768], P('mp'), may hold values from -0.15625 to 0.15625
- second_gain: bfloat16 [768], replicated, may hold values from 0.5 to 1.5
- router_weight: bfloat16 [768, 8], replicated, may hold values from -0.109375 to 0.109375
- expert_up: bfloat16 [8, 768, 3072], P('dp', None, 'mp'), may hold values from -0.21875 to 0.21875
- up_bias: bfloat16 [8, 3072], P('dp', 'mp'), may hold values from -0.59765625 to 0.59765625
- expert_down: bfloat16 [8, 3072, 768], P('dp', 'mp'), may hold values from -2 to 2
- down_bias: bfloat16 [8, 768], P('dp'), may hold values from -2.65625 to 2.65625
Outputs:
- block_out: bfloat16 [8192, 768], P('dp')
- token_grad: float32 [8192, 768], P('dp')
- first_gain_grad: float32 [768], replicated
- mixer_in_grad: float32 [768, 2, 1536], P(None, None, 'mp')
- conv_weight_grad: float32 [4, 1536], P(None, 'mp')
- conv_bias_grad: float32 [1536], P('mp')
- select_weight_grad: float32 [1536, 80], P('mp')
- step_weight_grad: float32 [48, 1536], P(None, 'mp')
- step_bias_grad: float32 [1536], P('mp')
- decay_log_grad: float32 [16, 1536], P(None, 'mp')
- skip_gain_grad: float32 [1536], P('mp')
- mixer_out_grad: float32 [1536, 768], P('mp')
- second_gain_grad: float32 [768], replicated
- router_weight_grad: float32 [768, 8], replicated
- expert_up_grad: float32 [8, 768, 3072], P('dp', None, 'mp')
- up_bias_grad: float32 [8, 3072], P('dp', 'mp')
- expert_down_grad: float32 [8, 3072, 768], P('dp', 'mp')
- down_bias_grad: float32 [8, 768], P('dp')
Inputs may be any that keep to these rules, and one draw needn't show every extreme that they name: `lengths`: each entry is a sequence's valid places, counted from place 0; at least one sequence has all 2048.
All inputs are finite; a program needn't handle non-finite values.
Results may differ from a plain program's by a relative error of at most 0.017.
Values may be sent and summed in bfloat16 or wider, within the bound.
A program may use at most 448 MiB of HBM per device.

v0:
```python
import functools

import jax
import jax.numpy as jnp
from jax import lax
from jax.experimental import pallas as pl
from jax.experimental.pallas import tpu as pltpu
from jax.sharding import PartitionSpec as P

F32 = jnp.float32
BF16 = jnp.bfloat16
SLOT_DEV = 256
LANES = 128
SUB = 8
LOG2E = 1.4426950408889634
LN2 = 0.6931471805599453
VMEM = 48 * 2**20
norm_eps = 1e-05


def lane(col):
    return jnp.broadcast_to(col, (SUB, LANES))


def row(ref, n, cs):
    return jnp.broadcast_to(ref[n : n + 1, cs], (SUB, LANES))


def tiles(count):
    return [slice(ct * LANES, (ct + 1) * LANES) for ct in range(count // LANES)]


def whole(*dims):
    return pl.BlockSpec(dims, lambda i: (0,) * len(dims))


def local_forward_kernel(step_ref, x_ref, bin_ref, rates_ref, out_ref):
    places, chans = step_ref.shape[0], step_ref.shape[2]
    states, half = rates_ref.shape[0], 8
    cols = tiles(chans)
    for nh in range(states // half):
        ns = [nh * half + n for n in range(half)]

        def body(i, st):
            st = list(st)
            b = bin_ref[i]
            bb = [lane(b[:, n : n + 1]) for n in ns]
            for ct, cs in enumerate(cols):
                s = step_ref[i, :, cs]
                x = x_ref[i, :, cs]
                for n in range(half):
                    k = n * len(cols) + ct
                    e = jnp.exp2(s * row(rates_ref, ns[n], cs))
                    st[k] = e * st[k] + x * bb[n]
            return tuple(st)

        zero = tuple(jnp.zeros((SUB, LANES), F32) for _ in range(half * len(cols)))
        st = lax.fori_loop(0, places, body, zero, unroll=8)
        for n in range(half):
            for ct, cs in enumerate(cols):
                out_ref[ns[n], :, cs] = st[n * len(cols) + ct]


def local_forward(step, x, bin_vals, rates):
    return pl.pallas_call(
        local_forward_kernel,
        out_shape=jax.ShapeDtypeStruct((rates.shape[0], SUB, step.shape[2]), F32),
        compiler_params=pltpu.CompilerParams(vmem_limit_bytes=VMEM),
    )(step, x, bin_vals, rates)


def forward_kernel(
    step_ref, x_ref, bin_ref, cout_ref, rates_ref, h0_ref, y_ref, hb_ref, hf_ref, st_ref
):
    places, chans = step_ref.shape[0], step_ref.shape[2]
    states, half = rates_ref.shape[0], 8
    cols = tiles(chans)

    @pl.when(pl.program_id(0) == 0)
    def _():
        st_ref[...] = h0_ref[...]

    for nh in range(states // half):
        ns = [nh * half + n for n in range(half)]

        def body(i, st):
            st = list(st)
            b = bin_ref[i]
            c = cout_ref[i]
            bb = [lane(b[:, n : n + 1]) for n in ns]
            cc = [lane(c[:, n : n + 1]) for n in ns]
            for ct, cs in enumerate(cols):
                s = step_ref[i, :, cs]
                x = x_ref[i, :, cs]
                y = y_ref[i, :, cs] if nh else jnp.zeros((SUB, LANES), F32)
                for n in range(half):
                    k = n * len(cols) + ct
                    hb_ref[i, ns[n], :, cs] = st[k].astype(hb_ref.dtype)
                    e = jnp.exp2(s * row(rates_ref, ns[n], cs))
                    st[k] = e * st[k] + x * bb[n]
                    y = y + cc[n] * st[k]
                y_ref[i, :, cs] = y
            return tuple(st)

        st = tuple(st_ref[n, :, cs] for n in ns for cs in cols)
        st = lax.fori_loop(0, places, body, st, unroll=8)
        for n in range(half):
            for ct, cs in enumerate(cols):
                st_ref[ns[n], :, cs] = st[n * len(cols) + ct]
    hf_ref[...] = st_ref[...]


def forward(step, x, bin_vals, cout, rates, h0, block=16):
    places, _, chans = step.shape
    states = rates.shape[0]
    part = lambda width: pl.BlockSpec((block, SUB, width), lambda i: (i, 0, 0))
    return pl.pallas_call(
        forward_kernel,
        grid=(places // block,),
        in_specs=[
            part(chans),
            part(chans),
            part(states),
            part(states),
            whole(states, chans),
            whole(states, SUB, chans),
        ],
        out_specs=[
            part(chans),
            pl.BlockSpec((block, states, SUB, chans), lambda i: (i, 0, 0, 0)),
            whole(states, SUB, chans),
        ],
        out_shape=[
            jax.ShapeDtypeStruct((places, SUB, chans), F32),
            jax.ShapeDtypeStruct((places, states, SUB, chans), BF16),
            jax.ShapeDtypeStruct((states, SUB, chans), F32),
        ],
        scratch_shapes=[pltpu.VMEM((states, SUB, chans), F32)],
        compiler_params=pltpu.CompilerParams(vmem_limit_bytes=VMEM),
    )(step, x, bin_vals, cout, rates, h0)


def local_backward_kernel(step_ref, gs_ref, cout_ref, rates_ref, out_ref):
    places, chans = step_ref.shape[0], step_ref.shape[2]
    states, half = rates_ref.shape[0], 8
    cols = tiles(chans)
    for nh in range(states // half):
        ns = [nh * half + n for n in range(half)]

        def body(lap, st):
            i = places - 1 - lap
            st = list(st)
            c = cout_ref[i]
            cc = [lane(c[:, n : n + 1]) for n in ns]
            for ct, cs in enumerate(cols):
                s = step_ref[i, :, cs]
                g = gs_ref[i, :, cs]
                for n in range(half):
                    k = n * len(cols) + ct
                    e = jnp.exp2(s * row(rates_ref, ns[n], cs))
                    st[k] = e * (st[k] + g * cc[n])
            return tuple(st)

        zero = tuple(jnp.zeros((SUB, LANES), F32) for _ in range(half * len(cols)))
        st = lax.fori_loop(0, places, body, zero, unroll=8)
        for n in range(half):
            for ct, cs in enumerate(cols):
                out_ref[ns[n], :, cs] = st[n * len(cols) + ct]


def local_backward(step, gs, cout, rates):
    return pl.pallas_call(
        local_backward_kernel,
        out_shape=jax.ShapeDtypeStruct((rates.shape[0], SUB, step.shape[2]), F32),
        compiler_params=pltpu.CompilerParams(vmem_limit_bytes=VMEM),
    )(step, gs, cout, rates)


def backward_kernel(
    step_ref,
    x_ref,
    gs_ref,
    gp_ref,
    bin_ref,
    cout_ref,
    rates_ref,
    g0_ref,
    hb_ref,
    sg_ref,
    sb_ref,
    qb_ref,
    qc_ref,
    rt_out,
    gst_ref,
    rt_ref,
    q_ref,
    p_ref,
):
    places, chans = step_ref.shape[0], step_ref.shape[2]
    states, some = rates_ref.shape[0], 4
    cols = tiles(chans)

    @pl.when(pl.program_id(0) == 0)
    def _():
        gst_ref[...] = g0_ref[...]
        rt_ref[...] = jnp.zeros_like(rt_ref)

    for nq in range(states // some):
        ns = [nq * some + n for n in range(some)]
        size = some * len(cols)

        def body(lap, carry):
            i = places - 1 - lap
            st, rt = list(carry[:size]), list(carry[size:])
            b = bin_ref[i]
            c = cout_ref[i]
            bb = [lane(b[:, n : n + 1]) for n in ns]
            cc = [lane(c[:, n : n + 1]) for n in ns]
            qb, qc = [None] * some, [None] * some
            for ct, cs in enumerate(cols):
                s = step_ref[i, :, cs]
                x = x_ref[i, :, cs]
                g = gs_ref[i, :, cs]
                gp = gp_ref[i, :, cs]
                sg = sg_ref[i, :, cs] if nq else jnp.zeros((SUB, LANES), F32)
                sb = sb_ref[i, :, cs] if nq else jnp.zeros((SUB, LANES), F32)
                for n in range(some):
                    k = n * len(cols) + ct
                    rate = row(rates_ref, ns[n], cs)
                    e = jnp.exp2(s * rate)
                    h = hb_ref[i, ns[n], :, cs].astype(F32)
                    grad = st[k] + g * cc[n]
                    st[k] = e * grad
                    dg = st[k] * h
                    sg = sg + dg * rate
                    rt[k] = rt[k] + dg * s
                    sb = sb + grad * bb[n]
                    qb[n] = grad * x if ct == 0 else qb[n] + grad * x
                    qc[n] = gp * h if ct == 0 else qc[n] + gp * h
                sg_ref[i, :, cs] = sg
                sb_ref[i, :, cs] = sb
            rows = pl.ds(pl.multiple_of(i * SUB, SUB), SUB)
            for n in range(some):
                q_ref[rows, ns[n] * LANES : (ns[n] + 1) * LANES] = qb[n]
                p_ref[rows, ns[n] * LANES : (ns[n] + 1) * LANES] = qc[n]
            return tuple(st) + tuple(rt)

        at = [(ns[n], slice(None), cs) for n in range(some) for cs in cols]
        init = tuple(gst_ref[a] for a in at) + tuple(rt_ref[a] for a in at)
        out = lax.fori_loop(0, places, body, init, unroll=8)
        for j, a in enumerate(at):
            gst_ref[a] = out[j]
            rt_ref[a] = out[size + j]
    dims = (states * LANES, states)
    sel = lax.broadcasted_iota(jnp.int32, dims, 0) // LANES == lax.broadcasted_iota(
        jnp.int32, dims, 1
    )
    sel = sel.astype(BF16)
    qb_ref[...] = jnp.dot(q_ref[...].astype(BF16), sel, preferred_element_type=F32)
    qc_ref[...] = jnp.dot(p_ref[...].astype(BF16), sel, preferred_element_type=F32)
    rt_out[...] = rt_ref[...]


def backward(step, x, gs, gp, bin_vals, cout, rates, g0, hb, block=16):
    places, _, chans = step.shape
    states = rates.shape[0]
    count = places // block
    part = lambda width: pl.BlockSpec((block, SUB, width), lambda i: (count - 1 - i, 0, 0))
    flat = pl.BlockSpec((block * SUB, states), lambda i: (count - 1 - i, 0))
    return pl.pallas_call(
        backward_kernel,
        grid=(count,),
        in_specs=[
            part(chans),
            part(chans),
            part(chans),
            part(chans),
            part(states),
            part(states),
            whole(states, chans),
            whole(states, SUB, chans),
            pl.BlockSpec((block, states, SUB, chans), lambda i: (count - 1 - i, 0, 0, 0)),
        ],
        out_specs=[part(chans), part(chans), flat, flat, whole(states, SUB, chans)],
        out_shape=[
            jax.ShapeDtypeStruct((places, SUB, chans), F32),
            jax.ShapeDtypeStruct((places, SUB, chans), F32),
            jax.ShapeDtypeStruct((places * SUB, states), F32),
            jax.ShapeDtypeStruct((places * SUB, states), F32),
            jax.ShapeDtypeStruct((states, SUB, chans), F32),
        ],
        scratch_shapes=[
            pltpu.VMEM((states, SUB, chans), F32),
            pltpu.VMEM((states, SUB, chans), F32),
            pltpu.VMEM((block * SUB, states * LANES), F32),
            pltpu.VMEM((block * SUB, states * LANES), F32),
        ],
        compiler_params=pltpu.CompilerParams(vmem_limit_bytes=VMEM),
    )(step, x, gs, gp, bin_vals, cout, rates, g0, hb)


def passed_along(block, axis, distance):
    devices = range(lax.axis_size(axis))
    route = [(i - distance, i) for i in devices if i - distance in devices]
    return lax.ppermute(block, axis, route)


def sum_mp(block):
    return lax.psum(block, "mp")


def entering_states(total, part, rates, reverse):
    count = lax.axis_size("dp")
    place = lax.axis_index("dp")
    ahead = count - 1 - place if reverse else place
    totals = lax.all_gather(total, "dp")
    parts = lax.all_gather(part.astype(BF16), "dp")

    def one(lap, state):
        source = count - 1 - lap if reverse else lap
        decay = jnp.exp2(
            rates[:, None, :] * lax.dynamic_index_in_dim(totals, source, 0, False)[None]
        )
        return decay * state + lax.dynamic_index_in_dim(parts, source, 0, False).astype(F32)

    return lax.fori_loop(0, ahead, one, jnp.zeros(part.shape, F32))


def silu_slope(values):
    sigmoid_vals = jax.nn.sigmoid(values)
    return sigmoid_vals * (1.0 + values * (1.0 - sigmoid_vals))


def gelu_tanh(values):
    return jax.nn.gelu(values, approximate=True)


def norm_back(grad_norm, normed, inverse, norm_gain):
    scaled = grad_norm * norm_gain
    return inverse * (scaled - normed * jnp.mean(scaled * normed, axis=-1, keepdims=True))


def dot(a, b, dims):
    return lax.dot_general(a, b, (dims, ((), ())), preferred_element_type=F32)


NN = ((1,), (0,))
NT = ((1,), (1,))
TN = ((0,), (0,))


def per_device(
    tokens,
    routes,
    lengths,
    cotangent,
    first_gain,
    mixer_in,
    conv_weight,
    conv_bias,
    select_weight,
    step_weight,
    step_bias,
    decay_log,
    skip_gain,
    mixer_out,
    second_gain,
    router_weight,
    expert_up,
    up_bias,
    expert_down,
    down_bias,
):
    tok_count, model_width = tokens.shape
    kernel, chan_count = conv_weight.shape
    rank_size = step_weight.shape[0]
    state_size = decay_log.shape[0]
    expert_total = router_weight.shape[1]
    capacity = max(2, (5 * tok_count + 4 * expert_total - 1) // (4 * expert_total))
    slot_dev = SLOT_DEV
    seq_count = tok_count // slot_dev
    chunks = SUB // seq_count
    places_dev = slot_dev // chunks
    edge = kernel - 1
    device = lax.axis_index("dp")
    last = lax.axis_size("dp") - 1

    def reorder(values):
        width = values.shape[-1]
        return values.reshape(SUB, places_dev, width).transpose(1, 0, 2).reshape(tok_count, width)

    def restore(values):
        width = values.shape[-1]
        return values.reshape(places_dev, SUB, width).transpose(1, 0, 2).reshape(tok_count, width)

    rows = jnp.arange(tok_count)
    sub_ids = rows % SUB
    seq_ids = sub_ids // chunks
    local_place = (sub_ids % chunks) * places_dev + rows // SUB
    original = seq_ids * slot_dev + local_place
    places = device * slot_dev + local_place
    seq_length = jnp.sum(
        jnp.where(seq_ids[:, None] == jnp.arange(lengths.shape[0])[None], lengths[None], 0), axis=1
    )
    valid_mask = (places < seq_length).astype(F32)
    valid_col = valid_mask[:, None]
    even = (jnp.arange(SUB) % chunks == 0)[None, :, None]
    odd = (jnp.arange(SUB) % chunks == chunks - 1)[None, :, None]

    tok_vals = reorder(tokens).astype(F32)
    cot_low = reorder(cotangent)
    cot_vals = cot_low.astype(F32)
    route_ids = reorder(routes)[:, 0]

    expert_iota = jnp.arange(expert_total, dtype=jnp.int32)
    route_match = route_ids[:, None] == expert_iota[None]
    route_hot = route_match.astype(F32)
    live_hot = route_hot * valid_col
    before = (original[None, :] < original[:, None]).astype(BF16)
    earlier = dot(before, live_hot.astype(BF16), NN)
    position = jnp.sum(earlier * live_hot, axis=1).astype(jnp.int32)
    kept_mask = (valid_mask > 0.5) & (position < capacity)
    slot_ids = jnp.where(kept_mask, route_ids * capacity + position, -1)
    slot_iota = jnp.arange(expert_total * capacity, dtype=jnp.int32)
    dispatch = (slot_ids[None, :] == slot_iota[:, None]).astype(BF16)

    def to_experts(values):
        sent = dot(dispatch, values, NN).astype(BF16).reshape(expert_total, capacity, model_width)
        return lax.all_to_all(sent, "dp", split_axis=0, concat_axis=1, tiled=True)[0]

    def from_experts(values):
        back = lax.all_to_all(values[None], "dp", split_axis=1, concat_axis=0, tiled=True)
        return dot(dispatch, back.reshape(expert_total * capacity, model_width), TN)

    cot_rows = to_experts(cot_low)

    inverse_one = lax.rsqrt(jnp.mean(tok_vals * tok_vals, axis=-1, keepdims=True) + norm_eps)
    normed_one = tok_vals * inverse_one
    first_vals = first_gain.astype(F32)
    normed_in = (normed_one * first_vals).astype(BF16)
    mixer_in_flat = mixer_in.reshape(model_width, 2 * chan_count)
    both_in = dot(normed_in, mixer_in_flat, NN).astype(BF16)
    gate_pre = both_in[:, chan_count:].astype(F32)
    conv_seq = both_in[:, :chan_count].astype(F32).reshape(places_dev, SUB, chan_count)
    tail = conv_seq[places_dev - edge :]
    other_tail = passed_along(tail.astype(BF16), "dp", 1).astype(F32)
    lead_rows = jnp.where(even, jnp.roll(other_tail, 1 - chunks, axis=1), jnp.roll(tail, 1, axis=1))
    extended = jnp.concatenate([lead_rows, conv_seq], axis=0)
    conv_taps = conv_weight.astype(F32)
    conv_pre = jnp.zeros(conv_seq.shape, F32) + conv_bias.astype(F32)
    for offset in range(kernel):
        conv_pre = conv_pre + conv_taps[offset] * extended[offset : offset + places_dev]
    conv_pre = conv_pre.reshape(tok_count, chan_count)
    inner_vals = jax.nn.silu(conv_pre).astype(BF16)
    inner_f = inner_vals.astype(F32)
    projected = sum_mp(dot(inner_vals, select_weight, NN))
    low_rank = projected[:, :rank_size]
    bin_vals = projected[:, rank_size : rank_size + state_size]
    cout_vals = projected[:, rank_size + state_size :]
    low_high = low_rank.astype(BF16)
    low_rest = (low_rank - low_high.astype(F32)).astype(BF16)
    step_pre = dot(
        jnp.concatenate([low_high, low_rest], axis=1),
        jnp.concatenate([step_weight, step_weight], axis=0),
        NN,
    ) + step_bias.astype(F32)
    step_vals = valid_col * jax.nn.softplus(step_pre)
    decay_rates = -jnp.exp(decay_log.astype(F32))
    rates = decay_rates * LOG2E

    by_place = lambda values: values.reshape(places_dev, SUB, values.shape[-1])
    drive = step_vals * inner_f
    step_p, drive_p, bin_p, cout_p = map(by_place, (step_vals, drive, bin_vals, cout_vals))
    chunk_state = local_forward(step_p, drive_p, bin_p, rates)
    chunk_steps = jnp.sum(step_p, axis=0)
    chunk_decay = jnp.exp2(rates[:, None, :] * chunk_steps[None])
    split = lambda values: [values[..., k::chunks, :] for k in range(chunks)]
    joined = lambda parts: jnp.stack(parts, axis=2).reshape(parts[0].shape[0], SUB, chan_count)
    states, decays = split(chunk_state), split(chunk_decay)
    total = jnp.sum(chunk_steps.reshape(seq_count, chunks, chan_count), axis=1)
    summary = jnp.zeros_like(states[0])
    for k in range(chunks):
        summary = decays[k] * summary + states[k]
    state_in = [entering_states(total, summary, rates, False)]
    for k in range(chunks - 1):
        state_in.append(decays[k] * state_in[k] + states[k])
    scan_sum, states_before, last_states = forward(
        step_p, drive_p, bin_p, cout_p, rates, joined(state_in)
    )
    skip_vals = skip_gain.astype(F32)
    scan_out = scan_sum.reshape(tok_count, chan_count) + skip_vals * inner_f
    gate_act = jax.nn.silu(gate_pre)
    gated_vals = (scan_out * gate_act).astype(BF16)
    mixer_vals = sum_mp(dot(gated_vals, mixer_out, NN))
    residual = tok_vals + valid_col * mixer_vals
    inverse_two = lax.rsqrt(jnp.mean(residual * residual, axis=-1, keepdims=True) + norm_eps)
    normed_two = residual * inverse_two
    second_vals = second_gain.astype(F32)
    normed_out = (normed_two * second_vals).astype(BF16)
    logits = dot(normed_out, router_weight, NN)
    route_probs = jax.nn.softmax(logits, axis=-1)
    gate_prob = jnp.sum(route_probs * route_hot, axis=-1)

    expert_rows = to_experts(normed_out)
    own_hot = (expert_iota == device).astype(F32)
    row_probs = jnp.sum(
        jax.nn.softmax(dot(expert_rows, router_weight, NN), axis=-1) * own_hot, axis=-1
    )
    expert_grad = (row_probs[:, None] * cot_rows.astype(F32)).astype(BF16)
    up_mat, down_mat = expert_up[0], expert_down[0]
    hidden_pre = dot(expert_rows, up_mat, NN) + up_bias.astype(F32)
    hidden_act, gelu_pull = jax.vjp(gelu_tanh, hidden_pre)
    hidden_low = hidden_act.astype(BF16)
    result_part = dot(hidden_low, down_mat, NN)
    expert_result = (sum_mp(result_part) + down_bias.astype(F32)).astype(BF16)
    tok_result = from_experts(expert_result)
    block_out = (residual + gate_prob[:, None] * tok_result).astype(BF16)
    grad_down_bias = jnp.sum(expert_grad.astype(F32), axis=0)[None]
    grad_down = dot(hidden_low, expert_grad, TN)[None]
    grad_hidden = dot(expert_grad, down_mat, NT)
    grad_pre = gelu_pull(grad_hidden)[0].astype(BF16)
    grad_up_bias = jnp.sum(grad_pre.astype(F32), axis=0)[None]
    grad_up = dot(expert_rows, grad_pre, TN)[None]
    grad_rows = sum_mp(dot(grad_pre, up_mat, NT)).astype(BF16)
    grad_experts = from_experts(grad_rows)
    grad_gate = jnp.sum(cot_vals * tok_result, axis=-1)
    grad_logits = (grad_gate[:, None] * route_probs * (route_hot - gate_prob[:, None])).astype(BF16)
    grad_router = dot(normed_out, grad_logits, TN)
    grad_normed = grad_experts + dot(grad_logits, router_weight, NT)
    grad_second = jnp.sum(grad_normed * normed_two, axis=0)
    grad_resid = cot_vals + norm_back(grad_normed, normed_two, inverse_two, second_vals)
    grad_mixed = (valid_col * grad_resid).astype(BF16)
    grad_mixer_out = dot(gated_vals, grad_mixed, TN)
    grad_gated = dot(grad_mixed, mixer_out, NT)
    grad_scan = grad_gated * gate_act
    grad_gate_pre = grad_gated * scan_out * silu_slope(gate_pre)
    grad_skip = jnp.sum(grad_scan * inner_f, axis=0)

    gs_p = by_place(grad_scan)
    chunk_grad = split(local_backward(step_p, gs_p, cout_p, rates))
    back = jnp.zeros_like(chunk_grad[0])
    for k in reversed(range(chunks)):
        back = decays[k] * back + chunk_grad[k]
    grad_in = [entering_states(total, back, rates, True)]
    for k in reversed(range(1, chunks)):
        grad_in.insert(0, decays[k] * grad_in[0] + chunk_grad[k])
    gp_p = jnp.concatenate([jnp.zeros_like(gs_p[:1]), gs_p[:-1]], axis=0)
    rate_sum, state_bin, grad_bin, cout_shift, rate_parts = backward(
        step_p, drive_p, gs_p, gp_p, bin_p, cout_p, rates, joined(grad_in), states_before
    )
    rate_sum = rate_sum.reshape(tok_count, chan_count) * LN2
    state_bin = state_bin.reshape(tok_count, chan_count)
    last_cout = jnp.sum(gs_p[places_dev - 1][None] * last_states, axis=-1).T
    grad_cout = jnp.concatenate([cout_shift[SUB:], last_cout], axis=0)
    grad_decay_log = jnp.sum(rate_parts, axis=1) * decay_rates
    grad_step = rate_sum + inner_f * state_bin
    grad_inner = grad_scan * skip_vals + step_vals * state_bin
    grad_step_pre = grad_step * valid_col * jax.nn.sigmoid(step_pre)
    grad_step_bias = jnp.sum(grad_step_pre, axis=0)
    step_pre_low = grad_step_pre.astype(BF16)
    grad_step_weight = dot(low_high, step_pre_low, TN)
    grad_low_part = dot(step_pre_low, step_weight, NT)
    proj_part = jnp.concatenate([grad_low_part, grad_bin, grad_cout], axis=1)
    grad_proj = sum_mp(proj_part).astype(BF16)
    grad_select = dot(inner_vals, grad_proj, TN)
    grad_inner = grad_inner + dot(grad_proj, select_weight, NT)
    grad_conv = grad_inner * silu_slope(conv_pre)
    grad_conv_bias = jnp.sum(grad_conv, axis=0)
    grad_conv_seq = by_place(grad_conv)
    grad_taps = jnp.stack(
        [
            jnp.sum(grad_conv_seq * extended[offset : offset + places_dev], axis=(0, 1))
            for offset in range(kernel)
        ],
        axis=0,
    )
    head = grad_conv_seq[:edge]
    other_head = passed_along(head, "dp", -1)
    tail_rows = jnp.where(odd, jnp.roll(other_head, chunks - 1, axis=1), jnp.roll(head, -1, axis=1))
    grad_tail = jnp.concatenate([grad_conv_seq, tail_rows], axis=0)
    grad_conv_in = jnp.zeros(grad_conv_seq.shape, F32)
    for offset in range(kernel):
        lead = edge - offset
        grad_conv_in = grad_conv_in + conv_taps[offset] * grad_tail[lead : lead + places_dev]
    grad_both = jnp.concatenate(
        [grad_conv_in.reshape(tok_count, chan_count), grad_gate_pre], axis=1
    ).astype(BF16)
    grad_mixer_in = dot(normed_in, grad_both, TN)
    input_part = dot(grad_both, mixer_in_flat, NT)
    grad_normed_in = sum_mp(input_part.astype(BF16)).astype(F32)
    grad_first = jnp.sum(grad_normed_in * normed_one, axis=0)
    token_grad = grad_resid + norm_back(grad_normed_in, normed_one, inverse_one, first_vals)
    summed = lax.psum(
        (
            grad_first,
            grad_mixer_in,
            grad_taps,
            grad_conv_bias,
            grad_select,
            grad_step_weight,
            grad_step_bias,
            grad_decay_log,
            grad_skip,
            grad_mixer_out,
            grad_second,
            grad_router,
        ),
        "dp",
    )
    return (
        restore(block_out),
        restore(token_grad),
        summed[0],
        summed[1].reshape(mixer_in.shape),
        *summed[2:],
        grad_up,
        grad_up_bias,
        grad_down,
        grad_down_bias,
    )


def solution(mesh):
    return jax.shard_map(
        per_device,
        mesh=mesh,
        in_specs=(
            P("dp", None),
            P("dp", None),
            P(),
            P("dp", None),
            P(),
            P(None, None, "mp"),
            P(None, "mp"),
            P("mp"),
            P("mp", None),
            P(None, "mp"),
            P("mp"),
            P(None, "mp"),
            P("mp"),
            P("mp", None),
            P(),
            P(),
            P("dp", None, "mp"),
            P("dp", "mp"),
            P("dp", "mp", None),
            P("dp", None),
        ),
        out_specs=(
            P("dp", None),
            P("dp", None),
            P(),
            P(None, None, "mp"),
            P(None, "mp"),
            P("mp"),
            P("mp", None),
            P(None, "mp"),
            P("mp"),
            P(None, "mp"),
            P("mp"),
            P("mp", None),
            P(),
            P(),
            P("dp", None, "mp"),
            P("dp", "mp"),
            P("dp", "mp", None),
            P("dp", None),
        ),
        check_vma=False,
    )
```

profile of v0, /device:TPU:16, one launch (start us, length us, event | category | flops | bytes accessed | tf_op | source)
XLA Modules:
  0.0 1059.5 jit_solution(4825472414039535726)
XLA Ops:
  11.7 2.9 convolution_convert_fusion.1
  15.8 3.4 collective-permute-start
  20.1 2.2 collective-permute-done
  26.4 32.6 %all-reduce.12.cloned.1.call-done = f32[1024,80]{0,1:T(8,128)} async-done(((f32[1024,80]{0,1:T(8,128)}), f32[1024,80]{0,1:T(8,128)}) %all-reduce.12.cloned.1.call-update) | async-done | bytes 327696 | tf_op jit(solution)/shard_map/psum | solution.py:309
  60.0 2.4 bitcast_reduce_fusion
  65.6 2.6 fusion.55
  68.2 5.8 shard_map.331
  78.5 26.1 %all-gather.3 = f32[8,4,384]{2,1,0:T(4,128)S(1)} all-gather(f32[1,4,384]{2,1,0:T(4,128)S(1)} %bitcast.264), channel_id=2, replica_groups=mesh['dp'=8,'mp'=4] {'dp'}, dimensions={0}, use_global_device_ids=true | all-gather | bytes 55296 | tf_op jit(solution)/shard_map/all_gather | solution.py:316
  105.7 33.1 %all-gather.1 = bf16[128,4,384]{2,1,0:T(4,128)(2,1)} all-gather(bf16[16,4,384]{2,1,0:T(4,128)(2,1)S(1)} %add_convert_fusion.3), channel_id=3, replica_groups=mesh['dp'=8,'mp'=4] {'dp'}, dimensions={0}, use_global_device_ids=true | all-gather | bytes 442368 | tf_op jit(solution)/shard_map/all_gather | solution.py:317
  138.8 3.9 while.22
  145.2 11.1 %shard_map.332 = (f32[128,8,384]{2,1,0:T(8,128)S(1)}, bf16[128,16,8,384]{3,2,1,0:T(8,128)(2,1)}, f32[16,8,384]{2,1,0:T(8,128)S(1)}) custom-call(f32[128,8,384]{2,1,0:T(8,128)S(1)} %get-tuple-element.214.step_ref, f32[128,8,384]{2,1,0:T(8,128)S(1)} %copy-done.4, f32[128,8,16]{2,1,0:T(8,128)S(1)} %bitcast.232, f32[128,8,16]{2,1,0:T(8,128)S(1)} %bitcast.234, ...), custom_call_target="tpu_custom_call" | custom-call | tf_op jit(solution)/shard_map/pallas_call | solution.py:117
  158.4 2.6 fusion.154
  162.8 74.3 %all-reduce.14.cloned.1.call-done = f32[1024,768]{1,0:T(8,128)} async-done(((f32[1024,768]{1,0:T(8,128)}), f32[1024,768]{1,0:T(8,128)}) %all-reduce.14.cloned.1.call-update) | async-done | bytes 3145744 | tf_op jit(solution)/shard_map/psum | solution.py:309
  237.0 5.0 multiply_reduce_fusion.2
  243.7 3.7 fusion.16
  247.4 6.0 all-to-all-start
  253.4 5.4 fusion.17
  258.8 36.6 %all-to-all-done = bf16[8,160,768]{2,1,0:T(8,128)(2,1)} async-done(((bf16[8,160,768]{2,1,0:T(8,128)(2,1)}), bf16[8,160,768]{2,1,0:T(8,128)(2,1)}, u32[]{:S(2)}, u32[]{:S(2)}) %all-to-all-start) | async-done | bytes 1966112 | tf_op jit(solution)/shard_map/all_to_all | solution.py:429
  295.5 8.0 all-to-all-start.2
  303.5 2.2 fusion.150
  306.0 5.4 convolution_add_fusion
  311.4 33.8 %all-to-all-done.2 = bf16[8,160,768]{2,1,0:T(8,128)(2,1)} async-done(((bf16[8,160,768]{2,1,0:T(8,128)(2,1)}), bf16[8,160,768]{2,1,0:T(8,128)(2,1)}, u32[]{:S(2)}, u32[]{:S(2)}) %all-to-all-start.2) | async-done | bytes 1966112 | tf_op jit(solution)/shard_map/all_to_all | solution.py:429
  345.2 2.8 convert_reduce_fusion
  348.0 4.5 convert_reduce_fusion.1
  353.8 3.6 fusion.88
  357.4 71.7 %all-reduce.23 = bf16[1280,768]{1,0:T(8,128)(2,1)} all-reduce(f32[1280,768]{1,0:T(8,128)} %fusion.88), channel_id=1, replica_groups=mesh['dp'=8,'mp'=4] {'mp'}, use_global_device_ids=true, to_apply=%region_17.18 | all-reduce | flops 983040 | bytes 5898240 | tf_op jit(solution)/shard_map/psum | solution.py:309
  429.1 10.1 copy.139
  439.8 13.7 %reduce.17 = bf16[1280,768]{1,0:T(8,128)(2,1)} reduce(bf16[1280,1,768]{2,1,0:T(2,128)(2,1)} %bitcast.237, bf16[]{:T(256)} %broadcast.589), dimensions={1}, to_apply=%bitcast.217.reduce_sub_computation | reduce | bytes 3932162
  453.5 5.8 reshape.438
  459.3 7.7 all-to-all-start.3
  467.4 6.5 fusion.84
  474.6 81.3 %all-reduce.16.cloned.1.call-done = f32[1280,768]{1,0:T(8,128)} async-done(((f32[1280,768]{1,0:T(8,128)}), f32[1280,768]{1,0:T(8,128)}) %all-reduce.16.cloned.1.call-update) | async-done | bytes 3932176 | tf_op jit(solution)/shard_map/psum | solution.py:309
  555.8 2.4 fusion.33
  558.2 15.1 %copy.140 = bf16[1,1280,768]{2,0,1:T(2,128)(2,1)} copy(bf16[1,1280,768]{2,1,0:T(8,128)(2,1)S(1)} %fusion.33) | data formatting | bytes 3932160 | tf_op jit(solution)/shard_map/broadcast_in_dim | solution.py:432
  573.3 13.7 %reduce.18 = bf16[1280,768]{1,0:T(8,128)(2,1)} reduce(bf16[1280,1,768]{2,1,0:T(2,128)(2,1)} %bitcast.238, bf16[]{:T(256)} %broadcast.589), dimensions={1}, to_apply=%bitcast.218.reduce_sub_computation | reduce | bytes 3932162
  587.0 5.8 reshape.436
  592.8 6.2 all-to-all-start.1
  602.4 6.7 reshape.439
  609.1 6.2 fusion
  615.3 25.6 %all-to-all-done.1 = bf16[8,2,61440]{2,1,0:T(2,128)(2,1)} async-done(((bf16[8,2,61440]{2,1,0:T(2,128)(2,1)}), bf16[8,2,61440]{2,1,0:T(2,128)(2,1)}, u32[]{:S(2)}, u32[]{:S(2)}) %all-to-all-start.1) | async-done | bytes 1966112 | tf_op jit(solution)/shard_map/all_to_all | solution.py:432
  641.0 6.7 reshape.437
  647.7 5.9 fusion.22
  655.4 3.7 convert_add_fusion.2
  659.1 3.2 fusion.60
  662.4 6.0 shard_map.333
  671.4 29.3 %all-gather.2 = bf16[128,4,384]{2,1,0:T(4,128)(2,1)S(1)} all-gather(bf16[16,4,384]{2,1,0:T(4,128)(2,1)S(1)} %add_convert_fusion.2), channel_id=4, replica_groups=mesh['dp'=8,'mp'=4] {'dp'}, dimensions={0}, use_global_device_ids=true | all-gather | bytes 442368 | tf_op jit(solution)/shard_map/all_gather | solution.py:317
  703.0 24.3 %shard_map.334 = (f32[128,8,384]{2,1,0:T(8,128)S(1)}, f32[128,8,384]{2,1,0:T(8,128)S(1)}, f32[1024,16]{1,0:T(8,128)S(1)}, f32[1024,16]{1,0:T(8,128)S(1)}, f32[16,8,384]{2,1,0:T(8,128)S(1)}) custom-call(f32[128,8,384]{2,1,0:T(8,128)} %copy-done.2, f32[128,8,384]{2,1,0:T(8,128)} %copy-done.3, f32[128,8,384]{2,1,0:T(8,128)} %bitcast.230, ...), custom_call_target="tpu_custom_call" | custom-call | tf_op jit(solution)/shard_map/pallas_call | solution.py:270
  730.1 3.7 fusion.147
  737.1 13.8 %all-reduce.24 = bf16[1024,80]{0,1:T(8,128)(2,1)S(1)} all-reduce(f32[1024,80]{0,1:T(8,128)S(1)} %maximum_maximum_fusion), channel_id=1, replica_groups=mesh['dp'=8,'mp'=4] {'mp'}, use_global_device_ids=true, to_apply=%region_23.24 | all-reduce | flops 81920 | bytes 491520 | tf_op jit(solution)/shard_map/psum | solution.py:309
  751.8 4.7 fusion.145
  757.6 3.7 collective-permute-start.1
  763.8 3.8 fusion.97
  767.6 2.6 convolution_convert_fusion
  772.6 3.8 fusion.142
  776.4 38.5 %all-reduce.18.cloned.1.call-done = bf16[1024,768]{1,0:T(8,128)(2,1)} async-done(((bf16[1024,768]{1,0:T(8,128)(2,1)}), bf16[1024,768]{1,0:T(8,128)(2,1)}) %all-reduce.18.cloned.1.call-update) | async-done | bytes 1572880 | tf_op jit(solution)/shard_map/psum | solution.py:309
  814.9 5.3 fusion.23
  820.5 4.9 fusion.62
  825.4 3.0 copy.105
  830.3 4.7 convolution_bitcast_fusion.1
  837.8 3.5 convolution_bitcast_fusion
  845.7 2.6 copy.104
  848.3 42.5 %all-reduce.20.cloned.1.call-done = (f32[768]{0:T(1024)}, f32[4,384]{1,0:T(4,128)}, f32[384]{0:T(512)}, f32[384]{0:T(512)}, f32[16,384]{1,0:T(8,128)}, /*index=5*/f32[384]{0:T(512)}, f32[768]{0:T(1024)}, f32[768,8]{0,1:T(8,128)}) async-done(((f32[768]{0:T(1024)}, f32[4,384]{1,0:T(4,128)}, f32[384]{0:T(512)}, f32[384]{0:T(512)}, f32[16,384]{1,0:T(8,128)}, /*index=5*/f32[384]{0:T(512)}, f32[768]{0:T(1024)}, ...) | async-done | bytes 66064 | tf_op jit(solution)/shard_map/psum | solution.py:593
  890.8 149.5 %all-reduce.22.cloned.1.call-done = (f32[768,2,384]{2,1,0:T(2,128)}, f32[384,80]{0,1:T(8,128)}, f32[48,384]{1,0:T(8,128)}, f32[384,768]{1,0:T(8,128)}) async-done(((f32[768,2,384]{2,1,0:T(2,128)}, f32[384,80]{0,1:T(8,128)}, f32[48,384]{1,0:T(8,128)}, f32[384,768]{1,0:T(8,128)}), (f32[768,2,384]{2,1,0:T(2,128)}, f32[384,80]{0,1:T(8,128)}, f32[48,384]{1,0:T(8,128)}, ...) | async-done | bytes 3735568 | tf_op jit(solution)/shard_map/psum | solution.py:593
  1041.7 4.0 copy.177
  (381 shorter events, 75.2 us)
Async XLA Ops:
  7.2 340.8 %copy-start = (bf16[1,768,768]{2,1,0:T(8,128)(2,1)S(1)}, bf16[1,768,768]{2,1,0:T(8,128)(2,1)}, u32[]{:S(2)}) copy-start(bf16[1,768,768]{2,1,0:T(8,128)(2,1)} %param.42) | copy-start | bytes 3538948
  7.2 51.7 %all-reduce.12.cloned.1.call-start = ((), (), s32[]{:S(2)}) async-start(), calls=%async_computation.4 | async-start | bytes 655360 | tf_op jit(solution)/shard_map/psum | solution.py:309
  14.7 5.4 copy-start.111
  14.7 5.4 copy-start.112
  15.8 8.5 copy-start.31
  15.8 6.5 collective-permute-start
  19.3 5.0 copy-start.83
  19.3 5.0 copy-start.85
  19.3 5.0 copy-start.87
  19.4 6.9 copy-start.79
  24.3 35.7 %copy-start.77 = (bf16[48,384]{1,0:T(8,128)(2,1)S(1)}, bf16[48,384]{1,0:T(8,128)(2,1)}, u32[]{:S(2)}) copy-start(bf16[48,384]{1,0:T(8,128)(2,1)} %param.33) | copy-start | bytes 110596
  26.3 210.8 %all-reduce.14.cloned.1.call-start = ((), (), s32[]{:S(2)}) async-start(), calls=%async_computation.5 | async-start | bytes 6291456 | tf_op jit(solution)/shard_map/psum | solution.py:309
  68.2 594.2 %copy-start.2 = (f32[128,8,384]{2,1,0:T(8,128)}, f32[128,8,384]{2,1,0:T(8,128)S(1)}, u32[]{:S(2)}) copy-start(f32[128,8,384]{2,1,0:T(8,128)S(1)} %get-tuple-element.214.step_ref) | copy-start | bytes 4718596
  76.6 66.1 %copy-start.45 = (f32[16,4,384]{2,1,0:T(4,128)S(1)}, f32[16,4,384]{2,1,0:T(4,128)}, u32[]{:S(2)}) copy-start(f32[16,4,384]{2,1,0:T(4,128)} %slice.141) | copy-start | bytes 294916
  145.2 11.1 %copy-start.24 = (bf16[1024,384]{1,0:T(8,128)(2,1)S(1)}, bf16[1024,384]{1,0:T(8,128)(2,1)}, u32[]{:S(2)}) copy-start(bf16[1024,384]{1,0:T(8,128)(2,1)} %copy-done.23) | copy-start | bytes 2359300
  145.2 11.1 %copy-start.48 = (bf16[1024,768]{1,0:T(8,128)(2,1)S(1)}, bf16[1024,768]{1,0:T(8,128)(2,1)}, u32[]{:S(2)}) copy-start(bf16[1024,768]{1,0:T(8,128)(2,1)} %copy-done.47) | copy-start | bytes 4718596
  145.2 11.1 %copy-start.94 = (f32[384]{0:T(512)S(1)}, f32[384]{0:T(512)}, u32[]{:S(2)}) copy-start(f32[384]{0:T(512)} %convert_element_type.234) | copy-start | bytes 4612
  162.8 90.7 %copy-start.101 = (s32[1024]{0:T(1024)}, s32[1024]{0:T(1024)S(1)}, u32[]{:S(2)}) copy-start(s32[1024]{0:T(1024)S(1)} %add_select_fusion.3) | copy-start | bytes 12292
  247.4 48.1 %all-to-all-start = ((bf16[8,160,768]{2,1,0:T(8,128)(2,1)}), bf16[8,160,768]{2,1,0:T(8,128)(2,1)}, u32[]{:S(2)}, u32[]{:S(2)}) async-start(bf16[8,160,768]{2,1,0:T(8,128)(2,1)} %bitcast.249), calls=%async_computation | async-start | bytes 3932160 | tf_op jit(solution)/shard_map/all_to_all | solution.py:429
  295.5 8.0 copy-start.103
  295.5 8.1 copy-start.64
  295.5 49.7 %all-to-all-start.2 = ((bf16[8,160,768]{2,1,0:T(8,128)(2,1)}), bf16[8,160,768]{2,1,0:T(8,128)(2,1)}, u32[]{:S(2)}, u32[]{:S(2)}) async-start(bf16[8,160,768]{2,1,0:T(8,128)(2,1)} %bitcast.248), calls=%async_computation.2 | async-start | bytes 3932160 | tf_op jit(solution)/shard_map/all_to_all | solution.py:429
  305.9 5.5 copy-start.65
  348.0 5.8 copy-start.115
  459.3 133.5 %all-to-all-start.3 = ((bf16[8,2,61440]{2,1,0:T(2,128)(2,1)}), bf16[8,2,61440]{2,1,0:T(2,128)(2,1)}, u32[]{:S(2)}, u32[]{:S(2)}) async-start(bf16[8,2,61440]{2,1,0:T(2,128)(2,1)} %reshape.438), calls=%async_computation.3 | async-start | bytes 3932160 | tf_op jit(solution)/shard_map/all_to_all | solution.py:432
  467.0 88.8 %all-reduce.16.cloned.1.call-start = ((), (), s32[]{:S(2)}) async-start(), calls=%async_computation.6 | async-start | bytes 7864320 | tf_op jit(solution)/shard_map/psum | solution.py:309
  592.8 6.3 copy-start.62
  592.8 48.2 %all-to-all-start.1 = ((bf16[8,2,61440]{2,1,0:T(2,128)(2,1)}), bf16[8,2,61440]{2,1,0:T(2,128)(2,1)}, u32[]{:S(2)}, u32[]{:S(2)}) async-start(bf16[8,2,61440]{2,1,0:T(2,128)(2,1)} %reshape.436), calls=%async_computation.1 | async-start | bytes 3932160 | tf_op jit(solution)/shard_map/all_to_all | solution.py:432
  599.0 215.9 %all-reduce.18.cloned.1.call-start = ((), (), s32[]{:S(2)}) async-start(), calls=%async_computation.7 | async-start | bytes 3145728 | tf_op jit(solution)/shard_map/psum | solution.py:309
  602.4 6.8 copy-start.102
  647.7 5.9 copy-start.22
  647.7 5.9 copy-start.40
  647.7 5.9 copy-start.69
  734.2 16.7 %copy-start.26 = (bf16[1024,384]{1,0:T(8,128)(2,1)S(1)}, bf16[1024,384]{1,0:T(8,128)(2,1)}, u32[]{:S(2)}) copy-start(bf16[1024,384]{1,0:T(8,128)(2,1)} %copy-done.23) | copy-start | bytes 2359300
  735.6 16.2 %copy-start.6 = (f32[1024,384]{1,0:T(8,128)S(1)}, f32[1024,384]{1,0:T(8,128)}, u32[]{:S(2)}) copy-start(f32[1024,384]{1,0:T(8,128)} %copy-done.5) | copy-start | bytes 4718596
  735.6 16.2 %copy-start.71 = (bf16[384,80]{0,1:T(8,128)(2,1)S(1)}, bf16[384,80]{0,1:T(8,128)(2,1)}, u32[]{:S(2)}) copy-start(bf16[384,80]{0,1:T(8,128)(2,1)} %param.32) | copy-start | bytes 184324
  735.6 16.2 %copy-start.96 = (f32[384]{0:T(512)S(1)}, f32[384]{0:T(512)}, u32[]{:S(2)}) copy-start(f32[384]{0:T(512)} %convert_element_type.234) | copy-start | bytes 4612
  756.5 4.9 copy-start.34
  756.5 4.9 copy-start.58
  756.5 5.8 copy-start.16
  756.5 7.1 copy-start.113
  756.5 7.2 copy-start.84
  756.5 7.2 copy-start.86
  756.5 7.2 copy-start.88
  756.6 7.2 copy-start.90
  757.6 6.0 collective-permute-start.1
  762.3 5.3 copy-start.51
  762.3 5.3 copy-start.118
  770.2 120.6 %all-reduce.20.cloned.1.call-start = ((), (), s32[]{:S(2)}) async-start(), calls=%async_computation.8 | async-start | bytes 139264 | tf_op jit(solution)/shard_map/psum | solution.py:593
  772.6 42.4 %copy-start.74 = (f32[1024]{0:T(1024)S(1)}, f32[1024]{0:T(1024)}, u32[]{:S(2)}) copy-start(f32[1024]{0:T(1024)} %rsqrt.22) | copy-start | bytes 12292
  772.6 42.4 %copy-start.76 = (f32[768]{0:T(1024)S(1)}, f32[768]{0:T(1024)}, u32[]{:S(2)}) copy-start(f32[768]{0:T(1024)} %copy-done.75) | copy-start | bytes 9220
  776.4 44.1 %copy-start.54 = (bf16[1024,384]{1,0:T(8,128)(2,1)S(1)}, bf16[1024,384]{1,0:T(8,128)(2,1)}, u32[]{:S(2)}) copy-start(bf16[1024,384]{1,0:T(8,128)(2,1)} %copy-done.53) | copy-start | bytes 2359300
  820.2 220.1 %all-reduce.22.cloned.1.call-start = ((), (), s32[]{:S(2)}) async-start(), calls=%async_computation.9 | async-start | bytes 7471104 | tf_op jit(solution)/shard_map/psum | solution.py:593
  837.8 4.9 copy-start.28
  837.8 4.9 copy-start.39
  1041.6 5.3 copy-start.63
  1041.6 5.9 copy-start.67
  1041.6 6.6 copy-start.108
  1041.6 7.1 copy-start.82
  1041.6 7.7 copy-start.107
  1041.6 8.3 copy-start.52
  1041.7 10.5 copy-start.1
  1045.7 5.3 copy-start.100
  1045.7 5.9 copy-start.81
  (67 other events, 167.7 us)
Sparse Core Ops, SparseCore 0:
  26.4 32.4 all-reduce.11
  161.2 75.8 all-reduce.13
  474.0 81.7 all-reduce.15
  770.4 44.5 all-reduce.17
  820.3 70.4 all-reduce.19
  895.8 144.5 all-reduce.21
where the time goes:
time: 1070 us; the launch traced here: 1060 us
  waiting for transfers between devices  518 us (48%)
  blocking collectives  174 us (16%)
  local copies, waits for them, and re-layouts  103 us (10%)
  matrix products  87.2 us (8%)
  other arithmetic  77.6 us (7%)
  Pallas kernels  47.2 us (4%)
  starting transfers between devices  36 us (3%)
  between operations  15.9 us (1%)
    psum x4, waiting for transfers between devices, sum_mp(): return lax.psum(block, 'mp')  227 us
    psum x2, waiting for transfers between devices, per_device(): lax.psum((grad_first, grad_mixer_in, grad_taps, grad_conv_bias, grad_sele...  192 us
    dot_general x27, matrix products, dot(): return lax.dot_general(a, b, (dims, ((), ())), preferred_element_type=F32)  87.2 us
    psum x2, blocking collectives, sum_mp(): return lax.psum(block, 'mp')  85.5 us
    all_to_all x2, waiting for transfers between devices, to_experts(): lax.all_to_all(sent, 'dp', split_axis=0, concat_axis=1, tiled=True)[0]  70.4 us
    all_gather x2, blocking collectives, entering_states(): parts = lax.all_gather(part.astype(BF16), 'dp')  62.4 us
    unnamed x256, local copies, waits for them, and re-layouts  56 us
    unnamed x2, other arithmetic  27.5 us
  transfers between devices with their start and end apart: 12, of which 11 were waited for; matrix products, arithmetic and copies ran while one was open for 10% of the time, Pallas kernels for 0%

commit v1 on v0

--- a/solution.py
+++ b/solution.py
@@ -16,6 +16,16 @@
 LN2 = 0.6931471805599453
 VMEM = 48 * 2**20
 norm_eps = 1e-05
+MESH = pl.DeviceIdType.MESH
+
+
+NN = ((1,), (0,))
+NT = ((1,), (1,))
+TN = ((0,), (0,))
+
+
+def dot(a, b, dims):
+    return lax.dot_general(a, b, (dims, ((), ())), preferred_element_type=F32)
 
 
 def lane(col):
@@ -186,15 +196,24 @@
     rates_ref,
     g0_ref,
     hb_ref,
-    sg_ref,
-    sb_ref,
+    inner_ref,
+    slope_ref,
+    low_ref,
+    weight_ref,
+    skip_ref,
+    base_ref,
+    low_out,
     qb_ref,
     qc_ref,
     rt_out,
+    sw_ref,
+    sbias_ref,
     gst_ref,
     rt_ref,
     q_ref,
     p_ref,
+    sg_ref,
+    sb_ref,
 ):
     places, chans = step_ref.shape[0], step_ref.shape[2]
     states, some = rates_ref.shape[0], 4
@@ -204,6 +223,8 @@
     def _():
         gst_ref[...] = g0_ref[...]
         rt_ref[...] = jnp.zeros_like(rt_ref)
+        sw_ref[...] = jnp.zeros_like(sw_ref)
+        sbias_ref[...] = jnp.zeros_like(sbias_ref)
 
     for nq in range(states // some):
         ns = [nq * some + n for n in range(some)]
@@ -259,14 +280,26 @@
     qb_ref[...] = jnp.dot(q_ref[...].astype(BF16), sel, preferred_element_type=F32)
     qc_ref[...] = jnp.dot(p_ref[...].astype(BF16), sel, preferred_element_type=F32)
     rt_out[...] = rt_ref[...]
-
-
-def backward(step, x, gs, gp, bin_vals, cout, rates, g0, hb, block=16):
+    flat = lambda ref: ref[...].reshape(places * SUB, chans)
+    sb = flat(sb_ref)
+    base_ref[...] = flat(gs_ref) * skip_ref[...] + flat(step_ref) * sb
+    pre = (flat(sg_ref) * LN2 + inner_ref[...].astype(F32) * sb) * slope_ref[...]
+    sbias_ref[...] += jnp.sum(pre.reshape(places, SUB, chans), axis=0)
+    pre = pre.astype(BF16)
+    sw_ref[...] += dot(low_ref[...], pre, TN)
+    low_out[...] = dot(pre, weight_ref[...], NT)
+
+
+def backward(
+    step, x, gs, gp, bin_vals, cout, rates, g0, hb, inner, slope, low, weight, skip, block=16
+):
     places, _, chans = step.shape
     states = rates.shape[0]
+    rank = weight.shape[0]
     count = places // block
     part = lambda width: pl.BlockSpec((block, SUB, width), lambda i: (count - 1 - i, 0, 0))
-    flat = pl.BlockSpec((block * SUB, states), lambda i: (count - 1 - i, 0))
+    flat = lambda width: pl.BlockSpec((block * SUB, width), lambda i: (count - 1 - i, 0))
+    rows = places * SUB
     return pl.pallas_call(
         backward_kernel,
         grid=(count,),
@@ -280,23 +313,40 @@
             whole(states, chans),
             whole(states, SUB, chans),
             pl.BlockSpec((block, states, SUB, chans), lambda i: (count - 1 - i, 0, 0, 0)),
+            flat(chans),
+            flat(chans),
+            flat(rank),
+            whole(rank, chans),
+            whole(1, chans),
         ],
-        out_specs=[part(chans), part(chans), flat, flat, whole(states, SUB, chans)],
+        out_specs=[
+            flat(chans),
+            flat(rank),
+            flat(states),
+            flat(states),
+            whole(states, SUB, chans),
+            whole(rank, chans),
+            whole(SUB, chans),
+        ],
         out_shape=[
-            jax.ShapeDtypeStruct((places, SUB, chans), F32),
-            jax.ShapeDtypeStruct((places, SUB, chans), F32),
-            jax.ShapeDtypeStruct((places * SUB, states), F32),
-            jax.ShapeDtypeStruct((places * SUB, states), F32),
+            jax.ShapeDtypeStruct((rows, chans), F32),
+            jax.ShapeDtypeStruct((rows, rank), F32),
+            jax.ShapeDtypeStruct((rows, states), F32),
+            jax.ShapeDtypeStruct((rows, states), F32),
             jax.ShapeDtypeStruct((states, SUB, chans), F32),
+            jax.ShapeDtypeStruct((rank, chans), F32),
+            jax.ShapeDtypeStruct((SUB, chans), F32),
         ],
         scratch_shapes=[
             pltpu.VMEM((states, SUB, chans), F32),
             pltpu.VMEM((states, SUB, chans), F32),
             pltpu.VMEM((block * SUB, states * LANES), F32),
             pltpu.VMEM((block * SUB, states * LANES), F32),
+            pltpu.VMEM((block, SUB, chans), F32),
+            pltpu.VMEM((block, SUB, chans), F32),
         ],
         compiler_params=pltpu.CompilerParams(vmem_limit_bytes=VMEM),
-    )(step, x, gs, gp, bin_vals, cout, rates, g0, hb)
+    )(step, x, gs, gp, bin_vals, cout, rates, g0, hb, inner, slope, low, weight, skip)
 
 
 def passed_along(block, axis, distance):
@@ -305,25 +355,736 @@
     return lax.ppermute(block, axis, route)
 
 
-def sum_mp(block):
-    return lax.psum(block, "mp")
-
-
-def entering_states(total, part, rates, reverse):
-    count = lax.axis_size("dp")
-    place = lax.axis_index("dp")
-    ahead = count - 1 - place if reverse else place
-    totals = lax.all_gather(total, "dp")
-    parts = lax.all_gather(part.astype(BF16), "dp")
-
-    def one(lap, state):
-        source = count - 1 - lap if reverse else lap
-        decay = jnp.exp2(
-            rates[:, None, :] * lax.dynamic_index_in_dim(totals, source, 0, False)[None]
+def mp_pair():
+    j = lax.axis_index("mp")
+    return j, j + 1 - 2 * (j % 2), (j + 2) % 4
+
+
+def greet(others):
+    barrier = pltpu.get_barrier_semaphore()
+    for other in others:
+        pl.semaphore_signal(barrier, inc=1, device_id=other, device_id_type=MESH)
+    pl.semaphore_wait(barrier, len(others))
+
+
+def sending(src, dst, send, recv, device):
+    copy = pltpu.make_async_remote_copy(
+        src_ref=src, dst_ref=dst, send_sem=send, recv_sem=recv, device_id=device, device_id_type=MESH
+    )
+    copy.start()
+    return copy
+
+
+def vmem_call(kernel, out_shape, scratch, collective_id, *args, cost=0):
+    space = pl.BlockSpec(memory_space=pltpu.VMEM)
+    return pl.pallas_call(
+        kernel,
+        out_shape=out_shape,
+        in_specs=[space] * len(args),
+        out_specs=jax.tree.map(lambda _: space, out_shape),
+        scratch_shapes=scratch,
+        compiler_params=pltpu.CompilerParams(
+            collective_id=collective_id, has_side_effects=True, vmem_limit_bytes=VMEM
+        ),
+    )(*args)
+
+
+def sum_kernel(count, x_ref, out_ref, ra, sb, rb, send, recv):
+    j, near, far = mp_pair()
+    near, far = {"mp": near}, {"mp": far}
+    half = x_ref.shape[0] // 2
+    size = half // count
+    own = pl.multiple_of((j % 2) * half, half)
+    other = pl.multiple_of((1 - j % 2) * half, half)
+    greet([near, far])
+    first = [
+        sending(x_ref.at[pl.ds(other + k * size, size)], ra.at[k], send.at[0, k], recv.at[0, k], near)
+        for k in range(count)
+    ]
+    second, third = [], []
+    for k in range(count):
+        first[k].wait_recv()
+        mine = x_ref[pl.ds(own + k * size, size), :].astype(F32)
+        sb[k] = (mine + ra[k].astype(F32)).astype(sb.dtype)
+        second.append(sending(sb.at[k], rb.at[k], send.at[1, k], recv.at[1, k], far))
+    for k in range(count):
+        second[k].wait_recv()
+        rows = pl.ds(own + k * size, size)
+        out_ref[rows, :] = (sb[k].astype(F32) + rb[k].astype(F32)).astype(out_ref.dtype)
+        third.append(
+            sending(out_ref.at[rows], out_ref.at[rows], send.at[2, k], recv.at[2, k], near)
         )
-        return decay * state + lax.dynamic_index_in_dim(parts, source, 0, False).astype(F32)
-
-    return lax.fori_loop(0, ahead, one, jnp.zeros(part.shape, F32))
+    for k in range(count):
+        third[k].wait_recv()
+    for copy in first + second + third:
+        copy.wait_send()
+
+
+def sum_mp(x, collective_id, count=4):
+    rows, width = x.shape
+    slots = pltpu.VMEM((count, rows // 2 // count, width), x.dtype)
+    sems = pltpu.SemaphoreType.DMA((3, count))
+    return vmem_call(
+        functools.partial(sum_kernel, count),
+        jax.ShapeDtypeStruct(x.shape, x.dtype),
+        [slots, slots, slots, sems, sems],
+        collective_id,
+        x,
+    )
+
+
+def half_turn(tile):
+    return pltpu.roll(tile, SUB // 2, 0)
+
+
+def exchange_kernel(n, reverse, part_ref, total_ref, rates_ref, packed_ref, *refs):
+    if reverse:
+        all_ref, out_ref, sbuf, rbuf, send, recv = refs
+    else:
+        out_ref, all_ref, sbuf, rbuf, send, recv = refs
+    g = lax.axis_index("dp")
+    states, chans = rates_ref.shape
+    pairs = states // 2
+    greet([{"dp": (g + k) % n} for k in range(1, n)])
+    upper = lax.broadcasted_iota(jnp.int32, (SUB, chans), 0) >= SUB // 2
+    total = total_ref[...]
+    copies = []
+    if not reverse:
+        all_ref[0] = total + half_turn(total)
+        copies += [
+            sending(all_ref.at[0], all_ref.at[k], send.at[1, k], recv.at[1, k], {"dp": (g + k) % n})
+            for k in range(1, n)
+        ]
+    decay = lambda m: jnp.exp2(jnp.broadcast_to(rates_ref[m : m + 1, :], (SUB, chans)) * total)
+
+    def summary(m):
+        part = part_ref[m]
+        return part + decay(m) * half_turn(part)
+
+    def packed(p):
+        low, high = summary(p), summary(p + pairs)
+        if reverse:
+            return jnp.where(upper, half_turn(high), low)
+        return jnp.where(upper, high, half_turn(low))
+
+    for p in range(0, pairs, 2):
+        sbuf[p * SUB : (p + 2) * SUB, :] = jnp.concatenate([packed(p), packed(p + 1)], axis=0).astype(BF16)
+    copies += [
+        sending(sbuf, rbuf.at[k], send.at[0, k], recv.at[0, k], {"dp": (g + k) % n})
+        for k in range(1, n)
+    ]
+    for copy in copies:
+        copy.wait_recv()
+
+    def one(lap, held):
+        away = n - 1 - lap
+        slot = n - away if reverse else away
+        use = (g + away < n) if reverse else (away <= g)
+        steps = all_ref[slot]
+        new = []
+        for p in range(0, pairs, 2):
+            got = rbuf[slot, p * SUB : (p + 2) * SUB, :].astype(F32)
+            for q in (p, p + 1):
+                fall = jnp.exp2(packed_ref[q] * steps)
+                value = fall * held[q] + got[(q - p) * SUB : (q - p + 1) * SUB]
+                new.append(jnp.where(use, value, held[q]))
+        return tuple(new)
+
+    zero = tuple(jnp.zeros((SUB, chans), F32) for _ in range(pairs))
+    held = lax.fori_loop(0, n - 1, one, zero)
+    for m in range(states):
+        state = held[m % pairs]
+        if (m >= pairs) != reverse:
+            state = half_turn(state)
+        later = half_turn(decay(m) * state + part_ref[m])
+        out_ref[m] = jnp.where(upper, state, later) if reverse else jnp.where(upper, later, state)
+    for copy in copies:
+        copy.wait_send()
+
+
+def exchange(n, reverse, collective_id, part, total, rates, *held):
+    states, chans = rates.shape
+    pairs = states // 2
+    wide = lambda r: jnp.broadcast_to(r[:, None, :], (pairs, SUB // 2, chans))
+    packed = jnp.concatenate([wide(rates[:pairs]), wide(rates[pairs:])], axis=1)
+    entering = jax.ShapeDtypeStruct((states, SUB, chans), F32)
+    totals = jax.ShapeDtypeStruct((n, SUB, chans), F32)
+    sems = pltpu.SemaphoreType.DMA((2, n))
+    return vmem_call(
+        functools.partial(exchange_kernel, n, reverse),
+        entering if reverse else [entering, totals],
+        [pltpu.VMEM((pairs * SUB, chans), BF16), pltpu.VMEM((n, pairs * SUB, chans), BF16), sems, sems],
+        collective_id,
+        part, total, rates, packed, *held,
+    )
+
+
+def spread(out_ref, n, g, y, c, near, far, arrived, send, recv):
+    hr, hc = out_ref.shape[1] // 2, out_ref.shape[2] // 2
+    at = lambda s, u: out_ref.at[s, pl.ds(pl.multiple_of(u * hr, hr), hr), pl.ds(pl.multiple_of(c * hc, hc), hc)]
+    outs, mids, ends = [], [], []
+
+    def first(k):
+        arrived(k)
+        s = (g + n - k) % n
+        mids.append(sending(at(s, y), at(s, y), send.at[1, k], recv.at[1, k], far))
+        outs.append(sending(at(s, y), at(s, y), send.at[2, k], recv.at[2, k], near))
+
+    def second(k):
+        s = (g + n - k) % n
+        mids[k].wait_recv()
+        ends.append(sending(at(s, 1 - y), at(s, 1 - y), send.at[3, k], recv.at[3, k], near))
+
+    def finish():
+        for copy in outs + ends:
+            copy.wait_recv()
+        for copy in outs + mids + ends:
+            copy.wait_send()
+
+    return first, second, finish
+
+
+def dispatch_kernel(n, x_ref, out_ref, send, recv, local):
+    g = lax.axis_index("dp")
+    j, near, far = mp_pair()
+    near, far = {"mp": near}, {"mp": far}
+    y, c = j // 2, j % 2
+    hr, hc = out_ref.shape[1] // 2, out_ref.shape[2] // 2
+    greet([near, far] + [{"dp": (g + k) % n} for k in range(1, n)])
+    rows = pl.ds(pl.multiple_of(y * hr, hr), hr)
+    place = out_ref.at[g, rows, pl.ds(pl.multiple_of(c * hc, hc), hc)]
+    own = pltpu.make_async_copy(x_ref.at[g], place, local)
+    own.start()
+    copies = [own] + [
+        sending(x_ref.at[(g + k) % n], place, send.at[0, k], recv.at[0, k], {"dp": (g + k) % n})
+        for k in range(1, n)
+    ]
+    arrived = lambda k: copies[k].wait_recv() if k else own.wait()
+    first, second, finish = spread(out_ref, n, g, y, c, near, far, arrived, send, recv)
+    for k in range(n + 1):
+        if k < n:
+            first(k)
+        if k >= 1:
+            second(k - 1)
+    finish()
+    for copy in copies[1:]:
+        copy.wait_send()
+
+
+def dispatch_rows(n, collective_id, x):
+    sems = pltpu.SemaphoreType.DMA((4, n))
+    return vmem_call(
+        functools.partial(dispatch_kernel, n),
+        jax.ShapeDtypeStruct((n, 2 * x.shape[1], 2 * x.shape[2]), x.dtype),
+        [sems, sems, pltpu.SemaphoreType.DMA],
+        collective_id, x,
+    )
+
+
+def return_kernel(n, count, bias_ref, *refs):
+    parts, refs = refs[:count], refs[count:]
+    outs, refs = refs[:count], refs[count:]
+    ra, sb, rb, qb, send, recv = refs
+    g = lax.axis_index("dp")
+    j, near, far = mp_pair()
+    near, far = {"mp": near}, {"mp": far}
+    y, c = j // 2, j % 2
+    rows, hr, hc = outs[0].shape[1], outs[0].shape[1] // 2, outs[0].shape[2] // 2
+    greet([near, far] + [{"dp": (g + k) % n} for k in range(1, n)])
+    mine = pl.ds(pl.multiple_of(c * hc, hc), hc)
+    theirs = pl.ds(pl.multiple_of((1 - c) * hc, hc), hc)
+    up = pl.ds(pl.multiple_of(y * hr, hr), hr)
+    down = pl.ds(pl.multiple_of((1 - y) * hr, hr), hr)
+    total = count * n
+    near_copies, far_copies, back_copies = [], [], []
+    for t in range(total):
+        a, k = t // n, t % n
+        to = (g + k) % n
+        near_copies.append(
+            sending(parts[a].at[to, :, theirs], ra.at[t], send.at[4, t], recv.at[4, t], near)
+        )
+
+    def pair_sum(t):
+        a, k = t // n, t % n
+        near_copies[t].wait_recv()
+        sb[t] = (parts[a][(g + k) % n, :, mine].astype(F32) + ra[t].astype(F32)).astype(BF16)
+        far_copies.append(sending(sb.at[t, down], rb.at[t], send.at[5, t], recv.at[5, t], far))
+
+    def full_sum(t):
+        a, k = t // n, t % n
+        far_copies[t].wait_recv()
+        value = sb[t, up, :].astype(F32) + rb[t].astype(F32)
+        if a == 0:
+            value = value + bias_ref[:, mine]
+        if k == 0:
+            outs[a][g, up, mine] = value.astype(BF16)
+            back_copies.append(None)
+        else:
+            to = (g + k) % n
+            qb[t] = value.astype(BF16)
+            back_copies.append(
+                sending(qb.at[t], outs[a].at[g, up, mine], send.at[0, t], recv.at[0, t], {"dp": to})
+            )
+
+    spreads = []
+    for a in range(count):
+        arrived = lambda k, a=a: back_copies[a * n + k].wait_recv() if k else None
+        spreads.append(
+            spread(outs[a], n, g, y, c, near, far, arrived, send.at[:, pl.ds(a * n, n)], recv.at[:, pl.ds(a * n, n)])
+        )
+    for t in range(total + 5):
+        if t < total:
+            pair_sum(t)
+        if 0 <= t - 1 < total:
+            full_sum(t - 1)
+        if 0 <= t - 3 < total:
+            spreads[(t - 3) // n][0]((t - 3) % n)
+        if 0 <= t - 5 < total:
+            spreads[(t - 5) // n][1]((t - 5) % n)
+    for _, _, finish in spreads:
+        finish()
+    for copy in near_copies + far_copies + [b for b in back_copies if b is not None]:
+        copy.wait_send()
+
+
+def return_rows(n, collective_id, bias, *parts):
+    _, rows, width = parts[0].shape
+    count = len(parts)
+    sems = pltpu.SemaphoreType.DMA((6, count * n))
+    return vmem_call(
+        functools.partial(return_kernel, n, count),
+        [jax.ShapeDtypeStruct(p.shape, BF16) for p in parts],
+        [
+            pltpu.VMEM((count * n, rows, width // 2), BF16),
+            pltpu.VMEM((count * n, rows, width // 2), BF16),
+            pltpu.VMEM((count * n, rows // 2, width // 2), BF16),
+            pltpu.VMEM((count * n, rows // 2, width // 2), BF16),
+            sems, sems,
+        ],
+        collective_id, bias, *parts,
+    )
+
+
+def total_kernel(n, x_ref, out_ref, ra, sb, rc, send, recv):
+    g = lax.axis_index("dp")
+    odd = g % 2
+    pair = {"dp": g + 1 - 2 * odd}
+    m = n // 2
+    z = g // 2
+    like = [{"dp": 2 * ((z + k) % m) + odd} for k in range(1, m)]
+    greet([pair] + like)
+    order = [(z + k) % m for k in range(1, m)] + [z]
+    first = [
+        sending(x_ref.at[2 * order[k] + 1 - odd], ra.at[k], send.at[0, k], recv.at[0, k], pair)
+        for k in range(m)
+    ]
+    second = []
+    for k in range(m):
+        first[k].wait_recv()
+        sb[k] = (x_ref[2 * order[k] + odd].astype(F32) + ra[k].astype(F32)).astype(BF16)
+        if k < m - 1:
+            second.append(sending(sb.at[k], rc.at[k], send.at[1, k], recv.at[1, k], like[k]))
+    value = sb[m - 1].astype(F32)
+    for copy in second:
+        copy.wait_recv()
+    for k in range(m - 1):
+        value = value + rc[k].astype(F32)
+    out_ref[g] = value.astype(BF16)
+    third = [
+        sending(out_ref.at[g], out_ref.at[g], send.at[2, k], recv.at[2, k], like[k]) for k in range(m - 1)
+    ]
+    fourth = [sending(out_ref.at[g], out_ref.at[g], send.at[3, 0], recv.at[3, 0], pair)]
+    for k in range(m - 1):
+        third[k].wait_recv()
+        b = 2 * ((z + m - 1 - k) % m) + odd
+        fourth.append(sending(out_ref.at[b], out_ref.at[b], send.at[3, k + 1], recv.at[3, k + 1], pair))
+    for copy in fourth:
+        copy.wait_recv()
+    for copy in first + second + third + fourth:
+        copy.wait_send()
+
+
+def total_dp(n, collective_id, x):
+    _, rows, width = x.shape
+    m = n // 2
+    slots = lambda count: pltpu.VMEM((count, rows, width), BF16)
+    sems = pltpu.SemaphoreType.DMA((4, m))
+    return vmem_call(
+        functools.partial(total_kernel, n),
+        jax.ShapeDtypeStruct(x.shape, BF16),
+        [slots(m), slots(m), slots(m), sems, sems],
+        collective_id, x,
+    )
+
+
+def ds(start, size):
+    return pl.ds(pl.multiple_of(start, size), size)
+
+
+def mixer_back_kernel(
+    n,
+    proj_ref,
+    select_ref,
+    inner_ref,
+    base_ref,
+    pre_ref,
+    both_ref,
+    lead_ref,
+    gate_ref,
+    normed_ref,
+    weight_ref,
+    taps_ref,
+    gsel_ref,
+    sums_ref,
+    gin_ref,
+    part_ref,
+    conv_s,
+    ext_s,
+    both_s,
+    got,
+    send,
+    recv,
+):
+    g = lax.axis_index("dp")
+    rows, chans = inner_ref.shape
+    kernel = taps_ref.shape[0]
+    edge = (kernel - 1) * SUB
+    before, after = {"dp": (g + n - 1) % n}, {"dp": (g + 1) % n}
+    greet([before, after])
+    size = 256
+    sums_ref[...] = jnp.zeros_like(sums_ref)
+    ext_s[0:edge, :] = lead_ref[...]
+
+    def conv_block(b):
+        at = ds(b * size, size)
+        grad = base_ref[at, :] + dot(proj_ref[at, :], select_ref[...], NT)
+        grad = grad * silu_slope(pre_ref[at, :])
+        conv_s[at, :] = grad
+        ext_s[pl.ds(pl.multiple_of(b * size + edge, SUB), size), :] = both_ref[at, 0:chans].astype(F32)
+
+    conv_block(0)
+    copy = sending(conv_s.at[0:edge], got, send, recv, before)
+
+    def rest(b, _):
+        conv_block(b)
+        return 0
+
+    lax.fori_loop(1, rows // size, rest, 0)
+    gsel_ref[...] = dot(proj_ref[...], inner_ref[...], TN)
+
+    def taps(b, _):
+        grad = conv_s[ds(b * size, size), :]
+        folded = lambda v: jnp.sum(v.reshape(size // SUB, SUB, chans), axis=0)
+        for k in range(kernel):
+            past = ext_s[pl.ds(pl.multiple_of(b * size + k * SUB, SUB), size), :]
+            sums_ref[k] += folded(grad * past)
+        sums_ref[kernel] += folded(grad)
+        return 0
+
+    lax.fori_loop(0, rows // size, taps, 0)
+    copy.wait_recv()
+    upper = lax.broadcasted_iota(jnp.int32, (SUB, chans), 0) >= SUB // 2
+    some = jnp.where(g < n - 1, 1.0, 0.0)
+    for k in range(kernel - 1):
+        at = slice(k * SUB, (k + 1) * SUB)
+        tail = half_turn(jnp.where(upper, conv_s[at, :], got[at, :] * some))
+        conv_s[rows + k * SUB : rows + (k + 1) * SUB, :] = tail
+
+    def back(b, _):
+        at = ds(b * size, size)
+        total = jnp.zeros((size, chans), F32)
+        for k in range(kernel):
+            later = conv_s[pl.ds(pl.multiple_of(b * size + (kernel - 1 - k) * SUB, SUB), size), :]
+            total = total + taps_ref[k : k + 1, :] * later
+        both_s[at, 0:chans] = total.astype(BF16)
+        both_s[at, chans : 2 * chans] = gate_ref[at, :]
+        part_ref[at, :] = dot(both_s[at, :], weight_ref[...], NT).astype(BF16)
+        return 0
+
+    lax.fori_loop(0, rows // size, back, 0)
+
+    def weights(b, _):
+        at = ds(b * size, size)
+        gin_ref[:, at] = dot(normed_ref[...], both_s[:, at], TN).astype(BF16)
+        return 0
+
+    lax.fori_loop(0, 2 * chans // size, weights, 0)
+    copy.wait_send()
+
+
+def mixer_back(n, collective_id, proj, select, inner, base, pre, both, lead, gate, normed, weight, taps):
+    rows, chans = inner.shape
+    width = normed.shape[1]
+    kernel = taps.shape[0]
+    edge = (kernel - 1) * SUB
+    shape = jax.ShapeDtypeStruct
+    return vmem_call(
+        functools.partial(mixer_back_kernel, n),
+        [
+            shape((select.shape[1], chans), F32),
+            shape((kernel + 1, SUB, chans), F32),
+            shape((width, 2 * chans), BF16),
+            shape((rows, width), BF16),
+        ],
+        [
+            pltpu.VMEM((rows + edge, chans), F32),
+            pltpu.VMEM((rows + edge, chans), F32),
+            pltpu.VMEM((rows, 2 * chans), BF16),
+            pltpu.VMEM((edge, chans), F32),
+            pltpu.SemaphoreType.DMA,
+            pltpu.SemaphoreType.DMA,
+        ],
+        collective_id, proj, select, inner, base, pre, both, lead, gate, normed, weight, taps,
+    )
+
+
+def token_back_kernel(
+    cuts,
+    slot_ref,
+    result_ref,
+    rows_ref,
+    residual_ref,
+    probs_ref,
+    hot_ref,
+    normed_ref,
+    cot_ref,
+    valid_ref,
+    gain_ref,
+    router_ref,
+    gated_ref,
+    out_ref,
+    scan_ref,
+    both_ref,
+    inner_ref,
+    block_ref,
+    resid_ref,
+    gs_ref,
+    gate_ref,
+    router_out,
+    second_ref,
+    mixer_ref,
+    skip_ref,
+    mixed_s,
+    block_s,
+):
+    rows, width = residual_ref.shape
+    chans = inner_ref.shape[1]
+    slots = result_ref.shape[0]
+    size = 256
+    router_out[...] = jnp.zeros_like(router_out)
+    second_ref[...] = jnp.zeros_like(second_ref)
+    skip_ref[...] = jnp.zeros_like(skip_ref)
+
+    def body(b, _):
+        at = ds(b * size, size)
+        folded = lambda v: jnp.sum(v.reshape(size // SUB, SUB, v.shape[1]), axis=0)
+        iota = lax.broadcasted_iota(jnp.int32, (size, slots), 1)
+        pick = jnp.where(iota == slot_ref[at, :], 1.0, 0.0).astype(BF16)
+        result = dot(pick, result_ref[...], NN)
+        grad = dot(pick, rows_ref[...], NN)
+        probs, hot = probs_ref[at, :], hot_ref[at, :]
+        chosen = jnp.sum(probs * hot, axis=1, keepdims=True)
+        residual = residual_ref[at, :]
+        block = residual + chosen * result
+        for ct in range(width // LANES):
+            block_s[ct, at, :] = block[:, ct * LANES : (ct + 1) * LANES]
+        cot = cot_ref[at, :].astype(F32)
+        gate = jnp.sum(cot * result, axis=1, keepdims=True)
+        logit = (gate * probs * (hot - chosen)).astype(BF16)
+        router_out[...] += dot(logit, normed_ref[at, :], TN)
+        grad = grad + dot(logit, router_ref[...], NT)
+        inverse = lax.rsqrt(jnp.mean(residual * residual, axis=1, keepdims=True) + norm_eps)
+        normed = residual * inverse
+        second_ref[...] += folded(grad * normed)
+        scaled = grad * gain_ref[...]
+        mean = jnp.mean(scaled * normed, axis=1, keepdims=True)
+        resid = cot + inverse * (scaled - normed * mean)
+        resid_ref[at, :] = resid
+        mixed = (valid_ref[at, :] * resid).astype(BF16)
+        mixed_s[at, :] = mixed
+        grad_gated = dot(mixed, out_ref[...], NT)
+        pre = both_ref[at, chans : 2 * chans].astype(F32)
+        sig = jax.nn.sigmoid(pre)
+        act = pre * sig
+        gs = grad_gated * act
+        gs_ref[at, :] = gs
+        skip_ref[...] += folded(gs * inner_ref[at, :].astype(F32))
+        gate_ref[at, :] = (grad_gated * scan_ref[at, :] * (sig * (1.0 + pre * (1.0 - sig)))).astype(BF16)
+        return 0
+
+    lax.fori_loop(0, rows // size, body, 0)
+    mixer_ref[...] = dot(gated_ref[...], mixed_s[...], TN)
+    restore(cuts, block_s, block_ref)
+
+
+def restore(cuts, tile_ref, out_ref):
+    seqs, chunks, places = cuts
+    for ct in range(tile_ref.shape[0]):
+        for q in range(seqs):
+            for k in range(chunks):
+                picked = tile_ref[ct, pl.ds(k * seqs + q, places, stride=SUB), :]
+                start = (q * chunks + k) * places
+                out_ref[start : start + places, ct * LANES : (ct + 1) * LANES] = picked.astype(out_ref.dtype)
+
+
+def token_back(cuts, *args):
+    (slot, result, _, residual, probs, _, _, _, _, _, router, gated, _, scan, both, inner) = args
+    rows, width = residual.shape
+    chans = inner.shape[1]
+    shape = jax.ShapeDtypeStruct
+    return pl.pallas_call(
+        functools.partial(token_back_kernel, cuts),
+        out_shape=[
+            shape((rows, width), BF16),
+            shape((rows, width), F32),
+            shape((rows, chans), F32),
+            shape((rows, chans), BF16),
+            shape((router.shape[1], width), F32),
+            shape((SUB, width), F32),
+            shape((chans, width), F32),
+            shape((SUB, chans), F32),
+        ],
+        scratch_shapes=[
+            pltpu.VMEM((rows, width), BF16),
+            pltpu.VMEM((width // LANES, rows, LANES), F32),
+        ],
+        compiler_params=pltpu.CompilerParams(vmem_limit_bytes=VMEM),
+    )(*args)
+
+
+def last_kernel(
+    n, count, cuts, x_ref, blocks_ref, tok_ref, resid_ref, gain_ref, grad_ref, out_ref, first_ref,
+    sum_s, ra, sb, rb, pa, ps, pc, tile_s, firsts, send, recv,
+):
+    g = lax.axis_index("dp")
+    j, near, far = mp_pair()
+    near, far = {"mp": near}, {"mp": far}
+    odd, z, m = g % 2, g // 2, n // 2
+    pair = {"dp": g + 1 - 2 * odd}
+    like = [{"dp": 2 * ((z + k) % m) + odd} for k in range(1, m)]
+    others = [{"dp": (g + k) % n} for k in range(1, n)]
+    greet([near, far] + others)
+    rows, width = x_ref.shape
+    half = rows // 2
+    size = half // count
+    own = (j % 2) * half
+    other = (1 - j % 2) * half
+    one = [
+        sending(x_ref.at[ds(other + k * size, size)], ra.at[k], send.at[0, k], recv.at[0, k], near)
+        for k in range(count)
+    ]
+    order = [(z + k) % m for k in range(1, m)] + [z]
+    first = [
+        sending(blocks_ref.at[2 * order[k] + 1 - odd], pa.at[k], send.at[3, k], recv.at[3, k], pair)
+        for k in range(m)
+    ]
+    two, three, second = [], [], []
+
+    def pair_sum(k):
+        first[k].wait_recv()
+        ps[k] = (blocks_ref[2 * order[k] + odd].astype(F32) + pa[k].astype(F32)).astype(BF16)
+        if k < m - 1:
+            second.append(sending(ps.at[k], pc.at[k], send.at[4, k], recv.at[4, k], like[k]))
+
+    for k in range(max(count, m)):
+        if k < count:
+            one[k].wait_recv()
+            mine = x_ref[ds(own + k * size, size), :].astype(F32)
+            sb[k] = (mine + ra[k].astype(F32)).astype(BF16)
+            two.append(sending(sb.at[k], rb.at[k], send.at[1, k], recv.at[1, k], far))
+        if k < m:
+            pair_sum(k)
+    firsts[0] = jnp.zeros(firsts.shape[1:], F32)
+    gain = gain_ref[...]
+
+    def norm_rows(start):
+        at = ds(start, size)
+        grad = sum_s[at, :].astype(F32)
+        tok = tok_ref[at, :].astype(F32)
+        inverse = lax.rsqrt(jnp.mean(tok * tok, axis=1, keepdims=True) + norm_eps)
+        normed = tok * inverse
+        firsts[0] += jnp.sum((grad * normed).reshape(size // SUB, SUB, width), axis=0)
+        scaled = grad * gain
+        mean = jnp.mean(scaled * normed, axis=1, keepdims=True)
+        value = resid_ref[at, :] + inverse * (scaled - normed * mean)
+        for ct in range(width // LANES):
+            tile_s[ct, at, :] = value[:, ct * LANES : (ct + 1) * LANES]
+
+    for k in range(count):
+        two[k].wait_recv()
+        at = ds(own + k * size, size)
+        sum_s[at, :] = (sb[k].astype(F32) + rb[k].astype(F32)).astype(BF16)
+        three.append(sending(sum_s.at[at], sum_s.at[at], send.at[2, k], recv.at[2, k], near))
+    value = ps[m - 1].astype(F32)
+    for copy in second:
+        copy.wait_recv()
+    for k in range(m - 1):
+        value = value + pc[k].astype(F32)
+    out_ref[g] = value.astype(BF16)
+    third = [
+        sending(out_ref.at[g], out_ref.at[g], send.at[5, k], recv.at[5, k], like[k]) for k in range(m - 1)
+    ]
+    fourth = [sending(out_ref.at[g], out_ref.at[g], send.at[6, 0], recv.at[6, 0], pair)]
+    for k in range(count):
+        norm_rows(own + k * size)
+    for k in range(count):
+        three[k].wait_recv()
+        norm_rows(other + k * size)
+    spread_first = [
+        sending(firsts.at[0], firsts.at[k], send.at[7, k], recv.at[7, k], others[k - 1]) for k in range(1, n)
+    ]
+    for k in range(m - 1):
+        third[k].wait_recv()
+        b = 2 * ((z + m - 1 - k) % m) + odd
+        fourth.append(sending(out_ref.at[b], out_ref.at[b], send.at[6, k + 1], recv.at[6, k + 1], pair))
+    restore(cuts, tile_s, grad_ref)
+    for copy in spread_first:
+        copy.wait_recv()
+
+    def one_first(d, total):
+        return total + firsts[(g + n - d) % n]
+
+    first_ref[...] = lax.fori_loop(0, n, one_first, jnp.zeros(first_ref.shape, F32))
+    for copy in fourth:
+        copy.wait_recv()
+    for copy in one + two + three + first + second + third + fourth + spread_first:
+        copy.wait_send()
+
+
+def last_sums(n, collective_id, cuts, x, blocks, tok, resid, gain, count=4):
+    rows, width = x.shape
+    m = n // 2
+    height = blocks.shape[1]
+    slots = pltpu.VMEM((count, rows // 2 // count, width), BF16)
+    parts = pltpu.VMEM((m, height, width), BF16)
+    sems = pltpu.SemaphoreType.DMA((8, max(n, count)))
+    shape = jax.ShapeDtypeStruct
+    return vmem_call(
+        functools.partial(last_kernel, n, count, cuts),
+        [shape((rows, width), F32), shape(blocks.shape, BF16), shape((SUB, width), F32)],
+        [
+            pltpu.VMEM((rows, width), BF16),
+            slots,
+            slots,
+            slots,
+            parts,
+            parts,
+            parts,
+            pltpu.VMEM((width // LANES, rows, LANES), F32),
+            pltpu.VMEM((n, SUB, width), F32),
+            sems,
+            sems,
+        ],
+        collective_id, x, blocks, tok, resid, gain,
+    )
+
+
+def round_kernel(x_ref, out_ref):
+    out_ref[...] = x_ref[...].astype(BF16)
+
+
+def rounded(x):
+    return pl.pallas_call(round_kernel, out_shape=jax.ShapeDtypeStruct(x.shape, BF16))(x)
 
 
 def silu_slope(values):
@@ -338,15 +1099,6 @@
 def norm_back(grad_norm, normed, inverse, norm_gain):
     scaled = grad_norm * norm_gain
     return inverse * (scaled - normed * jnp.mean(scaled * normed, axis=-1, keepdims=True))
-
-
-def dot(a, b, dims):
-    return lax.dot_general(a, b, (dims, ((), ())), preferred_element_type=F32)
-
-
-NN = ((1,), (0,))
-NT = ((1,), (1,))
-TN = ((0,), (0,))
 
 
 def per_device(
@@ -383,20 +1135,17 @@
     places_dev = slot_dev // chunks
     edge = kernel - 1
     device = lax.axis_index("dp")
-    last = lax.axis_size("dp") - 1
+    dp_count = lax.axis_size("dp")
 
     def reorder(values):
         width = values.shape[-1]
-        return values.reshape(SUB, places_dev, width).transpose(1, 0, 2).reshape(tok_count, width)
-
-    def restore(values):
-        width = values.shape[-1]
-        return values.reshape(places_dev, SUB, width).transpose(1, 0, 2).reshape(tok_count, width)
+        cut = values.reshape(seq_count, chunks, places_dev, width)
+        return cut.transpose(2, 1, 0, 3).reshape(tok_count, width)
 
     rows = jnp.arange(tok_count)
     sub_ids = rows % SUB
-    seq_ids = sub_ids // chunks
-    local_place = (sub_ids % chunks) * places_dev + rows // SUB
+    seq_ids = sub_ids % seq_count
+    local_place = (sub_ids // seq_count) * places_dev + rows // SUB
     original = seq_ids * slot_dev + local_place
     places = device * slot_dev + local_place
     seq_length = jnp.sum(
@@ -404,12 +1153,11 @@
     )
     valid_mask = (places < seq_length).astype(F32)
     valid_col = valid_mask[:, None]
-    even = (jnp.arange(SUB) % chunks == 0)[None, :, None]
-    odd = (jnp.arange(SUB) % chunks == chunks - 1)[None, :, None]
-
-    tok_vals = reorder(tokens).astype(F32)
+    opening = (jnp.arange(SUB) < seq_count)[None, :, None]
+
+    tok_low = reorder(tokens)
+    tok_vals = tok_low.astype(F32)
     cot_low = reorder(cotangent)
-    cot_vals = cot_low.astype(F32)
     route_ids = reorder(routes)[:, 0]
 
     expert_iota = jnp.arange(expert_total, dtype=jnp.int32)
@@ -420,19 +1168,23 @@
     earlier = dot(before, live_hot.astype(BF16), NN)
     position = jnp.sum(earlier * live_hot, axis=1).astype(jnp.int32)
     kept_mask = (valid_mask > 0.5) & (position < capacity)
-    slot_ids = jnp.where(kept_mask, route_ids * capacity + position, -1)
-    slot_iota = jnp.arange(expert_total * capacity, dtype=jnp.int32)
-    dispatch = (slot_ids[None, :] == slot_iota[:, None]).astype(BF16)
-
-    def to_experts(values):
-        sent = dot(dispatch, values, NN).astype(BF16).reshape(expert_total, capacity, model_width)
-        return lax.all_to_all(sent, "dp", split_axis=0, concat_axis=1, tiled=True)[0]
-
-    def from_experts(values):
-        back = lax.all_to_all(values[None], "dp", split_axis=1, concat_axis=0, tiled=True)
-        return dot(dispatch, back.reshape(expert_total * capacity, model_width), TN)
-
-    cot_rows = to_experts(cot_low)
+    room = (capacity + 31) // 32 * 32
+    slot_ids = jnp.where(kept_mask, route_ids * room + position, -1)
+    half_rows, half_cols = room // 2, model_width // 2
+    place_mp = lax.axis_index("mp")
+    quarter_iota = (
+        jnp.arange(expert_total)[:, None] * room
+        + (place_mp // 2) * half_rows
+        + jnp.arange(half_rows)[None]
+    ).reshape(-1, 1)
+    quarter = (slot_ids[None, :] == quarter_iota).astype(BF16)
+
+    def to_experts(values, collective_id):
+        part = lax.dynamic_slice_in_dim(values, (place_mp % 2) * half_cols, half_cols, 1)
+        sent = dot(quarter, part, NN).astype(BF16).reshape(expert_total, half_rows, half_cols)
+        return dispatch_rows(dp_count, collective_id, sent).reshape(dp_count * room, model_width)
+
+    cot_rows = to_experts(cot_low, 0)
 
     inverse_one = lax.rsqrt(jnp.mean(tok_vals * tok_vals, axis=-1, keepdims=True) + norm_eps)
     normed_one = tok_vals * inverse_one
@@ -444,7 +1196,7 @@
     conv_seq = both_in[:, :chan_count].astype(F32).reshape(places_dev, SUB, chan_count)
     tail = conv_seq[places_dev - edge :]
     other_tail = passed_along(tail.astype(BF16), "dp", 1).astype(F32)
-    lead_rows = jnp.where(even, jnp.roll(other_tail, 1 - chunks, axis=1), jnp.roll(tail, 1, axis=1))
+    lead_rows = jnp.roll(jnp.where(opening, tail, other_tail), seq_count, axis=1)
     extended = jnp.concatenate([lead_rows, conv_seq], axis=0)
     conv_taps = conv_weight.astype(F32)
     conv_pre = jnp.zeros(conv_seq.shape, F32) + conv_bias.astype(F32)
@@ -453,7 +1205,7 @@
     conv_pre = conv_pre.reshape(tok_count, chan_count)
     inner_vals = jax.nn.silu(conv_pre).astype(BF16)
     inner_f = inner_vals.astype(F32)
-    projected = sum_mp(dot(inner_vals, select_weight, NN))
+    projected = sum_mp(dot(inner_vals, select_weight, NN), 1, 2)
     low_rank = projected[:, :rank_size]
     bin_vals = projected[:, rank_size : rank_size + state_size]
     cout_vals = projected[:, rank_size + state_size :]
@@ -465,6 +1217,7 @@
         NN,
     ) + step_bias.astype(F32)
     step_vals = valid_col * jax.nn.softplus(step_pre)
+    step_slope = valid_col * jax.nn.sigmoid(step_pre)
     decay_rates = -jnp.exp(decay_log.astype(F32))
     rates = decay_rates * LOG2E
 
@@ -473,25 +1226,15 @@
     step_p, drive_p, bin_p, cout_p = map(by_place, (step_vals, drive, bin_vals, cout_vals))
     chunk_state = local_forward(step_p, drive_p, bin_p, rates)
     chunk_steps = jnp.sum(step_p, axis=0)
-    chunk_decay = jnp.exp2(rates[:, None, :] * chunk_steps[None])
-    split = lambda values: [values[..., k::chunks, :] for k in range(chunks)]
-    joined = lambda parts: jnp.stack(parts, axis=2).reshape(parts[0].shape[0], SUB, chan_count)
-    states, decays = split(chunk_state), split(chunk_decay)
-    total = jnp.sum(chunk_steps.reshape(seq_count, chunks, chan_count), axis=1)
-    summary = jnp.zeros_like(states[0])
-    for k in range(chunks):
-        summary = decays[k] * summary + states[k]
-    state_in = [entering_states(total, summary, rates, False)]
-    for k in range(chunks - 1):
-        state_in.append(decays[k] * state_in[k] + states[k])
+    state_in, totals = exchange(dp_count, False, 2, chunk_state, chunk_steps, rates)
     scan_sum, states_before, last_states = forward(
-        step_p, drive_p, bin_p, cout_p, rates, joined(state_in)
+        step_p, drive_p, bin_p, cout_p, rates, state_in
     )
     skip_vals = skip_gain.astype(F32)
     scan_out = scan_sum.reshape(tok_count, chan_count) + skip_vals * inner_f
     gate_act = jax.nn.silu(gate_pre)
     gated_vals = (scan_out * gate_act).astype(BF16)
-    mixer_vals = sum_mp(dot(gated_vals, mixer_out, NN))
+    mixer_vals = sum_mp(dot(gated_vals, mixer_out, NN).astype(BF16), 3).astype(F32)
     residual = tok_vals + valid_col * mixer_vals
     inverse_two = lax.rsqrt(jnp.mean(residual * residual, axis=-1, keepdims=True) + norm_eps)
     normed_two = residual * inverse_two
@@ -501,7 +1244,7 @@
     route_probs = jax.nn.softmax(logits, axis=-1)
     gate_prob = jnp.sum(route_probs * route_hot, axis=-1)
 
-    expert_rows = to_experts(normed_out)
+    expert_rows = to_experts(normed_out, 4)
     own_hot = (expert_iota == device).astype(F32)
     row_probs = jnp.sum(
         jax.nn.softmax(dot(expert_rows, router_weight, NN), axis=-1) * own_hot, axis=-1
@@ -511,108 +1254,141 @@
     hidden_pre = dot(expert_rows, up_mat, NN) + up_bias.astype(F32)
     hidden_act, gelu_pull = jax.vjp(gelu_tanh, hidden_pre)
     hidden_low = hidden_act.astype(BF16)
-    result_part = dot(hidden_low, down_mat, NN)
-    expert_result = (sum_mp(result_part) + down_bias.astype(F32)).astype(BF16)
-    tok_result = from_experts(expert_result)
-    block_out = (residual + gate_prob[:, None] * tok_result).astype(BF16)
+    result_part = dot(hidden_low, down_mat, NN).astype(BF16)
     grad_down_bias = jnp.sum(expert_grad.astype(F32), axis=0)[None]
     grad_down = dot(hidden_low, expert_grad, TN)[None]
     grad_hidden = dot(expert_grad, down_mat, NT)
     grad_pre = gelu_pull(grad_hidden)[0].astype(BF16)
     grad_up_bias = jnp.sum(grad_pre.astype(F32), axis=0)[None]
     grad_up = dot(expert_rows, grad_pre, TN)[None]
-    grad_rows = sum_mp(dot(grad_pre, up_mat, NT)).astype(BF16)
-    grad_experts = from_experts(grad_rows)
-    grad_gate = jnp.sum(cot_vals * tok_result, axis=-1)
-    grad_logits = (grad_gate[:, None] * route_probs * (route_hot - gate_prob[:, None])).astype(BF16)
-    grad_router = dot(normed_out, grad_logits, TN)
-    grad_normed = grad_experts + dot(grad_logits, router_weight, NT)
-    grad_second = jnp.sum(grad_normed * normed_two, axis=0)
-    grad_resid = cot_vals + norm_back(grad_normed, normed_two, inverse_two, second_vals)
-    grad_mixed = (valid_col * grad_resid).astype(BF16)
-    grad_mixer_out = dot(gated_vals, grad_mixed, TN)
-    grad_gated = dot(grad_mixed, mixer_out, NT)
-    grad_scan = grad_gated * gate_act
-    grad_gate_pre = grad_gated * scan_out * silu_slope(gate_pre)
-    grad_skip = jnp.sum(grad_scan * inner_f, axis=0)
+    rows_part = dot(grad_pre, up_mat, NT).astype(BF16)
+    by_group = lambda values: values.reshape(dp_count, room, model_width)
+    returned = return_rows(
+        dp_count, 5, down_bias.astype(F32), by_group(result_part), by_group(rows_part)
+    )
+    cuts = (seq_count, chunks, places_dev)
+    (
+        block_out,
+        grad_resid,
+        grad_scan,
+        grad_gate_low,
+        grad_router,
+        grad_second,
+        grad_mixer_out,
+        grad_skip,
+    ) = token_back(
+        cuts,
+        slot_ids[:, None],
+        *[back.reshape(expert_total * room, model_width) for back in returned],
+        residual,
+        route_probs,
+        route_hot,
+        normed_out,
+        cot_low,
+        valid_col,
+        second_vals[None],
+        router_weight,
+        gated_vals,
+        mixer_out,
+        scan_out,
+        both_in,
+        inner_vals,
+    )
 
     gs_p = by_place(grad_scan)
-    chunk_grad = split(local_backward(step_p, gs_p, cout_p, rates))
-    back = jnp.zeros_like(chunk_grad[0])
-    for k in reversed(range(chunks)):
-        back = decays[k] * back + chunk_grad[k]
-    grad_in = [entering_states(total, back, rates, True)]
-    for k in reversed(range(1, chunks)):
-        grad_in.insert(0, decays[k] * grad_in[0] + chunk_grad[k])
+    chunk_grad = local_backward(step_p, gs_p, cout_p, rates)
+    grad_in = exchange(dp_count, True, 6, chunk_grad, chunk_steps, rates, totals)
     gp_p = jnp.concatenate([jnp.zeros_like(gs_p[:1]), gs_p[:-1]], axis=0)
-    rate_sum, state_bin, grad_bin, cout_shift, rate_parts = backward(
-        step_p, drive_p, gs_p, gp_p, bin_p, cout_p, rates, joined(grad_in), states_before
-    )
-    rate_sum = rate_sum.reshape(tok_count, chan_count) * LN2
-    state_bin = state_bin.reshape(tok_count, chan_count)
+    grad_base, grad_low_part, grad_bin, cout_shift, rate_parts, grad_step_weight, grad_step_bias = backward(
+        step_p,
+        drive_p,
+        gs_p,
+        gp_p,
+        bin_p,
+        cout_p,
+        rates,
+        grad_in,
+        states_before,
+        inner_vals,
+        step_slope,
+        low_high,
+        step_weight,
+        skip_vals[None],
+    )
     last_cout = jnp.sum(gs_p[places_dev - 1][None] * last_states, axis=-1).T
     grad_cout = jnp.concatenate([cout_shift[SUB:], last_cout], axis=0)
     grad_decay_log = jnp.sum(rate_parts, axis=1) * decay_rates
-    grad_step = rate_sum + inner_f * state_bin
-    grad_inner = grad_scan * skip_vals + step_vals * state_bin
-    grad_step_pre = grad_step * valid_col * jax.nn.sigmoid(step_pre)
-    grad_step_bias = jnp.sum(grad_step_pre, axis=0)
-    step_pre_low = grad_step_pre.astype(BF16)
-    grad_step_weight = dot(low_high, step_pre_low, TN)
-    grad_low_part = dot(step_pre_low, step_weight, NT)
     proj_part = jnp.concatenate([grad_low_part, grad_bin, grad_cout], axis=1)
-    grad_proj = sum_mp(proj_part).astype(BF16)
-    grad_select = dot(inner_vals, grad_proj, TN)
-    grad_inner = grad_inner + dot(grad_proj, select_weight, NT)
-    grad_conv = grad_inner * silu_slope(conv_pre)
-    grad_conv_bias = jnp.sum(grad_conv, axis=0)
-    grad_conv_seq = by_place(grad_conv)
-    grad_taps = jnp.stack(
-        [
-            jnp.sum(grad_conv_seq * extended[offset : offset + places_dev], axis=(0, 1))
-            for offset in range(kernel)
-        ],
-        axis=0,
-    )
-    head = grad_conv_seq[:edge]
-    other_head = passed_along(head, "dp", -1)
-    tail_rows = jnp.where(odd, jnp.roll(other_head, chunks - 1, axis=1), jnp.roll(head, -1, axis=1))
-    grad_tail = jnp.concatenate([grad_conv_seq, tail_rows], axis=0)
-    grad_conv_in = jnp.zeros(grad_conv_seq.shape, F32)
-    for offset in range(kernel):
-        lead = edge - offset
-        grad_conv_in = grad_conv_in + conv_taps[offset] * grad_tail[lead : lead + places_dev]
-    grad_both = jnp.concatenate(
-        [grad_conv_in.reshape(tok_count, chan_count), grad_gate_pre], axis=1
-    ).astype(BF16)
-    grad_mixer_in = dot(normed_in, grad_both, TN)
-    input_part = dot(grad_both, mixer_in_flat, NT)
-    grad_normed_in = sum_mp(input_part.astype(BF16)).astype(F32)
-    grad_first = jnp.sum(grad_normed_in * normed_one, axis=0)
-    token_grad = grad_resid + norm_back(grad_normed_in, normed_one, inverse_one, first_vals)
-    summed = lax.psum(
-        (
-            grad_first,
-            grad_mixer_in,
-            grad_taps,
-            grad_conv_bias,
-            grad_select,
-            grad_step_weight,
-            grad_step_bias,
-            grad_decay_log,
-            grad_skip,
-            grad_mixer_out,
-            grad_second,
-            grad_router,
-        ),
-        "dp",
-    )
+    grad_proj = sum_mp(proj_part.astype(BF16), 7, 2)
+    grad_select, conv_sums, grad_mixer_in, input_part = mixer_back(
+        dp_count,
+        8,
+        grad_proj,
+        select_weight,
+        inner_vals,
+        grad_base,
+        conv_pre,
+        both_in,
+        lead_rows.reshape(edge * SUB, chan_count),
+        grad_gate_low,
+        normed_in,
+        mixer_in_flat,
+        conv_taps,
+    )
+    conv_sums = jnp.sum(conv_sums, axis=1)
+    grad_taps, grad_conv_bias = conv_sums[:kernel], conv_sums[kernel]
+    shared = (
+        grad_mixer_in,
+        grad_mixer_out,
+        grad_select,
+        grad_step_weight,
+        grad_taps,
+        grad_conv_bias,
+        jnp.sum(grad_step_bias, axis=0),
+        grad_decay_log,
+        jnp.sum(grad_skip, axis=0),
+        jnp.sum(grad_second, axis=0),
+        grad_router,
+    )
+    flat = [part.reshape(-1) for part in shared[2:]]
+    rest = sum(part.size for part in flat)
+    height = (shared[0].size + shared[1].size + rest + model_width - 1) // model_width
+    height = (height + 16 * dp_count - 1) // (16 * dp_count) * (16 * dp_count)
+    pad = height * model_width - shared[0].size - shared[1].size - rest
+    small = jnp.concatenate(flat + [jnp.zeros((pad,), F32)]).reshape(-1, model_width)
+    stacked = jnp.concatenate([shared[0], rounded(jnp.concatenate([shared[1], small], axis=0))], axis=0)
+    token_grad, stacked, grad_first = last_sums(
+        dp_count,
+        9,
+        cuts,
+        input_part,
+        stacked.reshape(dp_count, -1, model_width),
+        tok_low,
+        grad_resid,
+        first_vals[None],
+    )
+    stacked = stacked.reshape(height, model_width).astype(F32)
+    first_rows, next_rows = shared[0].shape[0], shared[0].shape[0] + shared[1].shape[0]
+    tail_flat = stacked[next_rows:].reshape(-1)
+    summed, start = [stacked[:first_rows], stacked[first_rows:next_rows]], 0
+    for part in shared[2:]:
+        summed.append(tail_flat[start : start + part.size].reshape(part.shape))
+        start += part.size
     return (
-        restore(block_out),
-        restore(token_grad),
-        summed[0],
-        summed[1].reshape(mixer_in.shape),
-        *summed[2:],
+        block_out,
+        token_grad,
+        jnp.sum(grad_first, axis=0),
+        summed[0].reshape(mixer_in.shape),
+        summed[4],
+        summed[5],
+        summed[2].T,
+        summed[3],
+        summed[6],
+        summed[7],
+        summed[8],
+        summed[1],
+        summed[9],
+        summed[10].T,
         grad_up,
         grad_up_bias,
         grad_down,

time: 1070 us -> 498 us (0.47)
  waiting for transfers between devices: 518 us -> 0.01 us
  Pallas kernels: 47.2 us -> 338 us
  blocking collectives: 174 us -> 0 us
  matrix products: 87.2 us -> 30.8 us
  local copies, waits for them, and re-layouts: 103 us -> 69 us
  starting transfers between devices: 36 us -> 3.39 us
  other arithmetic: 77.6 us -> 47.8 us
  between operations: 15.9 us -> 2.63 us
    psum x6 -> x0, waiting for transfers between devices: 419 us -> none  [the longest x4 227 us: sum_mp(): return lax.psum(block, 'mp')]
    pallas_call x0 -> x12, Pallas kernels: none -> 290 us  [the longest x10 265 us: vmem_call(): pl.pallas_call(kernel, out_shape=out_shape, in_specs=[space] * len(args),...]
    all_to_all x4 -> x0, waiting for transfers between devices: 96.1 us -> none  [the longest x2 70.4 us: to_experts(): lax.all_to_all(sent, 'dp', split_axis=0, concat_axis=1, tiled=True)[0]]
    all_gather x3 -> x0, blocking collectives: 88.5 us -> none  [the longest x2 62.4 us: entering_states(): parts = lax.all_gather(part.astype(BF16), 'dp')]
    psum x2 -> x0, blocking collectives: 85.5 us -> none  [sum_mp(): return lax.psum(block, 'mp')]
    dot_general x27 -> x15, matrix products: 87.2 us -> 30.8 us  [dot(): return lax.dot_general(a, b, (dims, ((), ())), preferred_element_type=F32)]
    all_to_all x4 -> x0, starting transfers between devices: 27.9 us -> none  [the longest x2 14 us: to_experts(): lax.all_to_all(sent, 'dp', split_axis=0, concat_axis=1, tiled=True)[0]]
    unnamed x2 -> x0, other arithmetic: 27.5 us -> none
  transfers between devices with their start and end apart: 12 -> 1, of which waited for: 11 -> 0; matrix products, arithmetic and copies ran while one was open for 10% -> 6% of each run, Pallas kernels for 0% -> 5%
where the time goes in v1:
time: 498 us; the launch traced here: 491 us
  Pallas kernels  338 us (68%)
  local copies, waits for them, and re-layouts  69 us (14%)
  other arithmetic  47.8 us (10%)
  matrix products  30.8 us (6%)
    pallas_call x10, Pallas kernels, vmem_call(): pl.pallas_call(kernel, out_shape=out_shape, in_specs=[space] * len(args),...  265 us
    dot_general x15, matrix products, dot(): return lax.dot_general(a, b, (dims, ((), ())), preferred_element_type=F32)  30.8 us
    unnamed x240, local copies, waits for them, and re-layouts  29.9 us
    pallas_call x1, Pallas kernels, backward(): pl.pallas_call(backward_kernel, grid=(count,), in_specs=[part(chans), par...  25.2 us
    pallas_call x1, Pallas kernels, token_back(): pl.pallas_call(functools.partial(token_back_kernel, cuts), out_shape=[sha...  21.9 us
    pallas_call x1, Pallas kernels, forward(): pl.pallas_call(forward_kernel, grid=(places // block,), in_specs=[part(ch...  11.3 us
  transfers between devices with their start and end apart: 1, of which 0 were waited for; matrix products, arithmetic and copies ran while one was open for 6% of the time, Pallas kernels for 5%

profile of v1, /device:TPU:16, one launch (start us, length us, event | category | flops | bytes accessed | tf_op | source)
XLA Modules:
  0.0 491.5 jit_solution(4270530515836267233)
XLA Ops:
  0.7 2.8 fusion.16
  4.9 2.3 fusion.18
  7.2 1.3 convert_element_type.197
  8.5 1.6 copy.105
  10.3 1.4 convolution_convert_fusion.3.both_ref
  11.7 1.5 slice_convert_fusion
  13.2 1.1 copy-done.70
  14.4 3.4 collective-permute-start
  22.5 3.8 copy.112
  26.2 4.2 reshape.513.cot_ref
  34.1 2.7 add_select_fusion.2
  38.3 2.4 copy.113
  45.0 3.8 reshape.500.tok_ref
  48.8 23.1 %shard_map.337 = bf16[8,160,768]{2,1,0:T(8,128)(2,1)S(1)} custom-call(bf16[8,80,384]{2,1,0:T(8,128)(2,1)S(1)} %bitcast.119), custom_call_target="tpu_custom_call" | custom-call | tf_op jit(solution)/shard_map/pallas_call | solution.py:380
  71.9 1.3 copy-done.4
  76.2 1.5 pad_maximum_fusion.1
  77.7 2.7 multiply_convert_fusion.3
  80.8 11.0 %shard_map.331 = f32[1024,80]{1,0:T(8,128)S(1)} custom-call(f32[1024,80]{1,0:T(8,128)S(1)} %fusion.119.x_ref), custom_call_target="tpu_custom_call" | custom-call | tf_op jit(solution)/shard_map/pallas_call | solution.py:380
  92.5 2.4 divide_multiply_fusion
  96.2 5.9 %shard_map.332.part_ref = f32[16,8,384]{2,1,0:T(8,128)S(1)} custom-call(f32[128,8,384]{2,1,0:T(8,128)S(1)} %get-tuple-element.87.step_ref, f32[128,8,384]{2,1,0:T(8,128)S(1)} %get-tuple-element.95.x_ref, f32[128,8,16]{2,1,0:T(8,128)S(1)} %get-tuple-element.100.bin_ref, f32[16,384]{1,0:T(8,128)S(1)} %copy-done.28), custom_call_target="tpu_custom_call" | custom-call | tf_op jit(solution)/shard_map/pallas_call | solution.py:75
  102.1 15.4 %shard_map.333 = (f32[16,8,384]{2,1,0:T(8,128)S(1)}, f32[8,8,384]{2,1,0:T(8,128)S(1)}) custom-call(f32[16,8,384]{2,1,0:T(8,128)S(1)} %shard_map.332.part_ref, f32[8,384]{1,0:T(8,128)S(1)} %get-tuple-element.86.total_ref, f32[16,384]{1,0:T(8,128)S(1)} %copy-done.28, f32[8,8,384]{2,1,0:T(8,128)S(1)} %copy-done.33), custom_call_target="tpu_custom_call" | custom-call | tf_op jit(solution)/shard_map/pallas_call | solution.py:380
  118.1 11.3 %shard_map.334 = (f32[128,8,384]{2,1,0:T(8,128)S(1)}, bf16[128,16,8,384]{3,2,1,0:T(8,128)(2,1)}, f32[16,8,384]{2,1,0:T(8,128)S(1)}) custom-call(f32[128,8,384]{2,1,0:T(8,128)S(1)} %get-tuple-element.87.step_ref, f32[128,8,384]{2,1,0:T(8,128)S(1)} %get-tuple-element.95.x_ref, f32[128,8,16]{2,1,0:T(8,128)S(1)} %get-tuple-element.100.bin_ref, ...), custom_call_target="tpu_custom_call" | custom-call | tf_op jit(solution)/shard_map/pallas_call | solution.py:127
  129.5 1.8 fusion.33
  133.2 22.4 %shard_map.335 = bf16[1024,768]{1,0:T(8,128)(2,1)S(1)} custom-call(bf16[1024,768]{1,0:T(8,128)(2,1)S(1)} %convolution_convert_fusion.2.x_ref), custom_call_target="tpu_custom_call" | custom-call | tf_op jit(solution)/shard_map/pallas_call | solution.py:380
  155.6 2.5 multiply_reduce_fusion
  158.5 1.3 copy-done.62
  160.7 1.7 fusion.118
  162.4 24.6 %shard_map.336 = bf16[8,160,768]{2,1,0:T(8,128)(2,1)S(1)} custom-call(bf16[8,80,384]{2,1,0:T(8,128)(2,1)S(1)} %bitcast.120), custom_call_target="tpu_custom_call" | custom-call | tf_op jit(solution)/shard_map/pallas_call | solution.py:380
  187.1 1.3 copy-done.6
  189.7 1.4 mul.369
  191.1 3.4 fusion.9
  194.5 1.1 convert_reduce_fusion
  196.4 1.7 convolution_add_fusion
  198.1 4.5 convert_reduce_fusion.1
  202.6 3.2 convolution_bitcast_fusion.1
  205.7 3.0 convolution_convert_fusion
  208.8 3.7 convolution_convert_fusion.1
  213.5 1.1 fusion.78
  215.6 1.5 copy-done.26
  217.2 58.4 %shard_map.338 = (bf16[8,160,768]{2,1,0:T(8,128)(2,1)S(1)}, bf16[8,160,768]{2,1,0:T(8,128)(2,1)S(1)}) custom-call(f32[1,768]{1,0:T(1,128)S(1)} %copy-done.58, bf16[8,160,768]{2,1,0:T(8,128)(2,1)S(1)} %bitcast.118, bf16[8,160,768]{2,1,0:T(8,128)(2,1)} %bitcast.128), custom_call_target="tpu_custom_call" | custom-call | tf_op jit(solution)/shard_map/pallas_call | solution.py:380
  275.6 1.3 copy-done.24
  276.9 1.3 copy-done.25
  278.2 21.9 %shard_map.339 = (bf16[1024,768]{1,0:T(8,128)(2,1)}, f32[1024,768]{1,0:T(8,128)}, f32[1024,384]{1,0:T(8,128)}, bf16[1024,384]{1,0:T(8,128)(2,1)S(1)}, f32[8,768]...) custom-call(s32[1024,1]{1,0:T(8,128)S(1)} %copy-done.22, ...), custom_call_target="tpu_custom_call" | custom-call | tf_op jit(solution)/shard_map/pallas_call | solution.py:935
  300.2 1.8 slice_bitcast_fusion
  302.9 6.0 %shard_map.340.part_ref = f32[16,8,384]{2,1,0:T(8,128)S(1)} custom-call(f32[128,8,384]{2,1,0:T(8,128)S(1)} %get-tuple-element.87.step_ref, f32[128,8,384]{2,1,0:T(8,128)S(1)} %bitcast.113, f32[128,8,16]{2,1,0:T(8,128)S(1)} %copy-done.12, f32[16,384]{1,0:T(8,128)S(1)} %copy-done.29), custom_call_target="tpu_custom_call" | custom-call | tf_op jit(solution)/shard_map/pallas_call | solution.py:182
  309.0 12.3 %shard_map.341.g0_ref = f32[16,8,384]{2,1,0:T(8,128)S(1)} custom-call(f32[16,8,384]{2,1,0:T(8,128)S(1)} %shard_map.340.part_ref, f32[8,384]{1,0:T(8,128)S(1)} %get-tuple-element.86.total_ref, f32[16,384]{1,0:T(8,128)S(1)} %copy-done.29, f32[8,8,384]{2,1,0:T(8,128)S(1)} %copy-done.34, f32[8,8,384]{2,1,0:T(8,128)S(1)} %copy-done.51), custom_call_target="tpu_custom_call" | custom-call | tf_op jit(solution)/shard_map/pallas_call | solution.py:380
  321.3 1.2 concatenate.42.gp_ref
  322.6 25.2 %shard_map.342 = (f32[1024,384]{1,0:T(8,128)S(1)}, f32[1024,48]{1,0:T(8,128)S(1)}, f32[1024,16]{1,0:T(8,128)S(1)}, f32[1024,16]{1,0:T(8,128)S(1)}, f32[16,8,384]...) custom-call(f32[128,8,384]{2,1,0:T(8,128)} %copy-done.2, f32[128,8,384]{2,1,0:T(8,128)} %copy-done.3, ...), custom_call_target="tpu_custom_call" | custom-call | tf_op jit(solution)/shard_map/pallas_call | solution.py:303
  347.8 1.1 copy-done.32
  351.8 1.1 convert.18
  352.9 1.2 pad_maximum_fusion.3.x_ref
  354.1 7.4 %shard_map.343.proj_ref = bf16[1024,80]{1,0:T(8,128)(2,1)S(1)} custom-call(bf16[1024,80]{1,0:T(8,128)(2,1)S(1)} %pad_maximum_fusion.3.x_ref), custom_call_target="tpu_custom_call" | custom-call | tf_op jit(solution)/shard_map/pallas_call | solution.py:380
  361.5 1.1 copy-done.37
  363.4 13.8 %shard_map.344 = (f32[80,384]{1,0:T(8,128)S(1)}, f32[5,8,384]{2,1,0:T(8,128)S(1)}, bf16[768,768]{1,0:T(8,128)(2,1)S(1)}, bf16[1024,768]{1,0:T(8,128)(2,1)S(1)}) custom-call(bf16[1024,80]{1,0:T(8,128)(2,1)S(1)} %shard_map.343.proj_ref, bf16[384,80]{1,0:T(8,128)(2,1)S(1)} %copy-done.43, bf16[1024,384]{1,0:T(8,128)(2,1)S(1)} %get-tuple-element.90.inner_ref, ...), custom_call_target="tpu_custom_call" | custom-call | tf_op jit(solution)/shard_map/pallas_call | solution.py:380
  377.2 1.1 copy-done.30
  385.5 1.2 pad_maximum_fusion.2.x_ref
  386.8 2.4 shard_map.345
  389.1 2.7 pad_maximum_fusion
  391.8 76.9 %shard_map.346 = (f32[1024,768]{1,0:T(8,128)}, bf16[8,160,768]{2,1,0:T(8,128)(2,1)S(1)}, f32[8,768]{1,0:T(8,128)S(1)}) custom-call(bf16[1024,768]{1,0:T(8,128)(2,1)S(1)} %copy-done.31, bf16[8,160,768]{2,1,0:T(8,128)(2,1)} %bitcast.124, bf16[1024,768]{1,0:T(8,128)(2,1)S(1)} %copy-done.10, f32[1024,768]{1,0:T(8,128)} %get-tuple-element.72.resid_ref, ...), custom_call_target="tpu_custom_call" | custom-call | tf_op jit(solution)/shard_map/pallas_call | solution.py:380
  469.2 1.2 slice.184
  470.4 1.1 copy-done.65
  473.5 6.3 %convolution_bitcast_fusion = f32[1,768,768]{2,1,0:T(8,128)} fusion(bf16[1280,768]{1,0:T(8,128)(2,1)} %fusion.9, f32[1280,768]{1,0:T(8,128)} %copy-done.112), kind=kOutput, calls=%fused_computation.45 | convolution fusion | flops 1518796800 | bytes 8257536 | tf_op jit(solution)/shard_map/dot_general | solution.py:28
  479.9 2.3 reshape.527
  487.1 3.9 copy.124
  (329 shorter events, 47.7 us)
Async XLA Ops:
  0.7 197.4 %copy-start = (bf16[1,768,768]{2,1,0:T(8,128)(2,1)S(1)}, bf16[1,768,768]{2,1,0:T(8,128)(2,1)}, u32[]{:S(2)}) copy-start(bf16[1,768,768]{2,1,0:T(8,128)(2,1)} %param.38) | copy-start | bytes 3538948
  0.7 4.2 copy-start.66
  11.7 66.0 %copy-start.63 = (bf16[1024,768]{1,0:T(8,128)(2,1)}, bf16[1024,768]{1,0:T(8,128)(2,1)S(1)}, u32[]{:S(2)}) copy-start(bf16[1024,768]{1,0:T(8,128)(2,1)S(1)} %convolution_convert_fusion.3.both_ref) | copy-start | bytes 4718596
  11.7 6.1 %copy-start.96 = (s32[1024,1]{0,1:T(1,128)S(1)}, s32[1024,1]{0,1:T(1,128)}, u32[]{:S(2)}) copy-start(s32[1024,1]{0,1:T(1,128)} %param.21) | copy-start | bytes 12292
  11.7 6.5 %copy-start.110 = (s32[4]{0:T(128)S(1)}, s32[4]{0:T(128)}, u32[]{:S(2)}) copy-start(s32[4]{0:T(128)} %param.22) | copy-start | bytes 52
  14.4 60.9 %collective-permute-start = (bf16[3,8,384]{2,1,0:T(8,128)(2,1)S(1)}, bf16[3,8,384]{2,1,0:T(8,128)(2,1)S(1)}, u32[]{:S(2)}, u32[]{:S(2)}) collective-permute-start(bf16[3,8,384]{2,1,0:T(8,128)(2,1)S(1)} %fusion.91), channel_id=1, source_target_pairs={{0,4},{4,8},{8,12},{12,16},{16,20},{20,24},{24,28},{1,5},{5,9},{9,... | collective-permute-start | bytes 55304 | tf_op jit(solution)/shard_map/ppermute | solution.py:355
  18.0 3.7 copy-start.85
  18.3 7.9 %copy-start.83 = (f32[1024]{0:T(1024)}, f32[1024]{0:T(1024)S(1)}, u32[]{:S(2)}) copy-start(f32[1024]{0:T(1024)S(1)} %fusion.103) | copy-start | bytes 12292
  19.4 17.4 %copy-start.102 = (s32[1024]{0:T(1024)}, s32[1024]{0:T(1024)S(1)}, u32[]{:S(2)}) copy-start(s32[1024]{0:T(1024)S(1)} %add_select_fusion.7) | copy-start | bytes 12292
  22.5 14.3 %copy-start.100 = (s32[640]{0:T(1024)}, s32[640]{0:T(1024)S(1)}, u32[]{:S(2)}) copy-start(s32[640]{0:T(1024)S(1)} %add.325) | copy-start | bytes 7684
  26.2 4.2 copy-start.104
  37.7 3.7 copy-start.94
  37.7 4.9 copy-start.99
  37.7 6.1 %copy-start.107 = (bf16[384]{0:T(512)(128)(2,1)S(1)}, bf16[384]{0:T(512)(128)(2,1)}, u32[]{:S(2)}) copy-start(bf16[384]{0:T(512)(128)(2,1)} %param.27) | copy-start | bytes 2308
  37.7 6.7 %copy-start.108 = (bf16[384]{0:T(512)(128)(2,1)S(1)}, bf16[384]{0:T(512)(128)(2,1)}, u32[]{:S(2)}) copy-start(bf16[384]{0:T(512)(128)(2,1)} %param.30) | copy-start | bytes 2308
  48.8 24.4 %copy-start.105 = (bf16[1,768]{1,0:T(2,128)(2,1)S(1)}, bf16[1,768]{1,0:T(2,128)(2,1)}, u32[]{:S(2)}) copy-start(bf16[1,768]{1,0:T(2,128)(2,1)} %param.39) | copy-start | bytes 4612
  48.8 25.0 %copy-start.81 = (bf16[768,8]{0,1:T(8,128)(2,1)S(1)}, bf16[768,8]{0,1:T(8,128)(2,1)}, u32[]{:S(2)}) copy-start(bf16[768,8]{0,1:T(8,128)(2,1)} %param.35) | copy-start | bytes 36868
  48.8 25.8 %copy-start.75 = (bf16[384,80]{0,1:T(8,128)(2,1)S(1)}, bf16[384,80]{0,1:T(8,128)(2,1)}, u32[]{:S(2)}) copy-start(bf16[384,80]{0,1:T(8,128)(2,1)} %param.28) | copy-start | bytes 184324
  80.4 11.5 %copy-start.47 = (bf16[48,384]{1,0:T(8,128)(2,1)S(1)}, bf16[48,384]{1,0:T(8,128)(2,1)}, u32[]{:S(2)}) copy-start(bf16[48,384]{1,0:T(8,128)(2,1)} %weight_ref.1) | copy-start | bytes 110596
  80.4 11.5 %copy-start.93 = (f32[384]{0:T(512)S(1)}, f32[384]{0:T(512)}, u32[]{:S(2)}) copy-start(f32[384]{0:T(512)} %convert_element_type.206) | copy-start | bytes 4612
  94.9 23.2 %copy-start.3 = (f32[128,8,384]{2,1,0:T(8,128)}, f32[128,8,384]{2,1,0:T(8,128)S(1)}, u32[]{:S(2)}) copy-start(f32[128,8,384]{2,1,0:T(8,128)S(1)} %get-tuple-element.95.x_ref) | copy-start | bytes 4718596
  95.8 207.1 %copy-start.2 = (f32[128,8,384]{2,1,0:T(8,128)}, f32[128,8,384]{2,1,0:T(8,128)S(1)}, u32[]{:S(2)}) copy-start(f32[128,8,384]{2,1,0:T(8,128)S(1)} %get-tuple-element.87.step_ref) | copy-start | bytes 4718596
  96.2 22.0 %copy-start.11 = (f32[128,8,16]{2,1,0:T(8,128)}, f32[128,8,16]{2,1,0:T(8,128)S(1)}, u32[]{:S(2)}) copy-start(f32[128,8,16]{2,1,0:T(8,128)S(1)} %get-tuple-element.99.cout_ref) | copy-start | bytes 196612
  96.2 22.0 %copy-start.13 = (f32[128,8,16]{2,1,0:T(8,128)}, f32[128,8,16]{2,1,0:T(8,128)S(1)}, u32[]{:S(2)}) copy-start(f32[128,8,16]{2,1,0:T(8,128)S(1)} %get-tuple-element.100.bin_ref) | copy-start | bytes 196612
  96.2 5.9 %copy-start.33 = (f32[8,8,384]{2,1,0:T(8,128)S(1)}, f32[8,8,384]{2,1,0:T(8,128)}, u32[]{:S(2)}) copy-start(f32[8,8,384]{2,1,0:T(8,128)} %pad_maximum_fusion.4.packed_ref) | copy-start | bytes 294916
  118.1 11.4 %copy-start.64 = (bf16[1024,768]{1,0:T(8,128)(2,1)S(1)}, bf16[1024,768]{1,0:T(8,128)(2,1)}, u32[]{:S(2)}) copy-start(bf16[1024,768]{1,0:T(8,128)(2,1)} %copy-done.63) | copy-start | bytes 4718596
  118.1 11.4 %copy-start.92 = (f32[384]{0:T(512)S(1)}, f32[384]{0:T(512)}, u32[]{:S(2)}) copy-start(f32[384]{0:T(512)} %convert_element_type.209) | copy-start | bytes 4612
  133.2 22.4 %copy-start.9 = (bf16[1024,768]{1,0:T(8,128)(2,1)S(1)}, bf16[1024,768]{1,0:T(8,128)(2,1)}, u32[]{:S(2)}) copy-start(bf16[1024,768]{1,0:T(8,128)(2,1)} %reshape.500.tok_ref) | copy-start | bytes 4718596
  133.2 22.4 %copy-start.87 = (f32[768]{0:T(1024)S(1)}, f32[768]{0:T(1024)}, u32[]{:S(2)}) copy-start(f32[768]{0:T(1024)} %copy-done.86) | copy-start | bytes 9220
  133.2 22.4 %copy-start.89 = (f32[1024]{0:T(1024)S(1)}, f32[1024]{0:T(1024)}, u32[]{:S(2)}) copy-start(f32[1024]{0:T(1024)} %rsqrt.22) | copy-start | bytes 12292
  162.4 26.6 %copy-start.109 = (f32[8]{0:T(128)S(1)}, f32[8]{0:T(128)}, u32[]{:S(2)}) copy-start(f32[8]{0:T(128)} %compare_convert_fusion) | copy-start | bytes 100
  191.1 3.4 copy-start.5
  191.1 3.4 copy-start.88
  198.1 10.7 %copy-start.112 = (f32[1280,768]{1,0:T(8,128)}, f32[1280,768]{1,0:T(8,128)S(1)}, u32[]{:S(2)}) copy-start(f32[1280,768]{1,0:T(8,128)S(1)} %convolution_add_fusion) | copy-start | bytes 11796484
  212.5 3.1 copy-start.58
  217.1 61.0 %copy-start.18 = (bf16[1024,384]{1,0:T(8,128)(2,1)S(1)}, bf16[1024,384]{1,0:T(8,128)(2,1)}, u32[]{:S(2)}) copy-start(bf16[1024,384]{1,0:T(8,128)(2,1)} %copy-done.17) | copy-start | bytes 2359300
  217.1 61.0 %copy-start.21 = (f32[1024,8]{1,0:T(8,128)S(1)}, f32[1024,8]{1,0:T(8,128)}, u32[]{:S(2)}) copy-start(f32[1024,8]{1,0:T(8,128)} %fusion.74.hot_ref) | copy-start | bytes 98308
  217.1 61.0 %copy-start.22 = (s32[1024,1]{1,0:T(8,128)S(1)}, s32[1024,1]{1,0:T(8,128)}, u32[]{:S(2)}) copy-start(s32[1024,1]{1,0:T(8,128)} %get-tuple-element.92.slot_ref) | copy-start | bytes 12292
  217.1 61.0 %copy-start.23 = (f32[1024,1]{1,0:T(8,128)S(1)}, f32[1024,1]{1,0:T(8,128)}, u32[]{:S(2)}) copy-start(f32[1024,1]{1,0:T(8,128)} %get-tuple-element.93.valid_ref) | copy-start | bytes 12292
  217.1 61.0 %copy-start.35 = (bf16[768,8]{1,0:T(8,128)(2,1)S(1)}, bf16[768,8]{1,0:T(8,128)(2,1)}, u32[]{:S(2)}) copy-start(bf16[768,8]{1,0:T(8,128)(2,1)} %copy.98.router_ref) | copy-start | bytes 36868
  217.2 61.0 %copy-start.39 = (bf16[384,768]{1,0:T(8,128)(2,1)S(1)}, bf16[384,768]{1,0:T(8,128)(2,1)}, u32[]{:S(2)}) copy-start(bf16[384,768]{1,0:T(8,128)(2,1)} %out_ref.1) | copy-start | bytes 1769476
  217.2 61.0 %copy-start.57 = (f32[1,768]{1,0:T(1,128)S(1)}, f32[1,768]{1,0:T(1,128)}, u32[]{:S(2)}) copy-start(f32[1,768]{1,0:T(1,128)} %broadcast_in_dim.47.gain_ref) | copy-start | bytes 9220
  300.1 8.9 %copy-start.36 = (bf16[1024,384]{1,0:T(8,128)(2,1)}, bf16[1024,384]{1,0:T(8,128)(2,1)S(1)}, u32[]{:S(2)}) copy-start(bf16[1024,384]{1,0:T(8,128)(2,1)S(1)} %get-tuple-element.60.gate_ref) | copy-start | bytes 2359300
  300.1 8.9 %copy-start.59 = (f32[8,384]{1,0:T(8,128)}, f32[8,384]{1,0:T(8,128)S(1)}, u32[]{:S(2)}) copy-start(f32[8,384]{1,0:T(8,128)S(1)} %get-tuple-element.69) | copy-start | bytes 36868
  300.1 47.7 %copy-start.55 = (f32[8,768]{1,0:T(8,128)}, f32[8,768]{1,0:T(8,128)S(1)}, u32[]{:S(2)}) copy-start(f32[8,768]{1,0:T(8,128)S(1)} %get-tuple-element.71) | copy-start | bytes 73732
  300.1 47.7 %copy-start.56 = (f32[8,768]{1,0:T(8,128)}, f32[8,768]{1,0:T(8,128)S(1)}, u32[]{:S(2)}) copy-start(f32[8,768]{1,0:T(8,128)S(1)} %get-tuple-element.70) | copy-start | bytes 73732
  302.3 6.7 %copy-start.34 = (f32[8,8,384]{2,1,0:T(8,128)S(1)}, f32[8,8,384]{2,1,0:T(8,128)}, u32[]{:S(2)}) copy-start(f32[8,8,384]{2,1,0:T(8,128)} %pad_maximum_fusion.4.packed_ref) | copy-start | bytes 294916
  302.3 6.7 %copy-start.51 = (f32[8,8,384]{2,1,0:T(8,128)S(1)}, f32[8,8,384]{2,1,0:T(8,128)}, u32[]{:S(2)}) copy-start(f32[8,8,384]{2,1,0:T(8,128)} %copy-done.50) | copy-start | bytes 294916
  309.0 13.6 %copy-start.14 = (f32[128,8,16]{2,1,0:T(8,128)S(1)}, f32[128,8,16]{2,1,0:T(8,128)}, u32[]{:S(2)}) copy-start(f32[128,8,16]{2,1,0:T(8,128)} %copy-done.13) | copy-start | bytes 196612
  309.0 13.6 %copy-start.20 = (bf16[1024,48]{1,0:T(8,128)(2,1)S(1)}, bf16[1024,48]{1,0:T(8,128)(2,1)}, u32[]{:S(2)}) copy-start(bf16[1024,48]{1,0:T(8,128)(2,1)} %copy-done.19) | copy-start | bytes 294916
  309.0 13.6 %copy-start.48 = (bf16[48,384]{1,0:T(8,128)(2,1)S(1)}, bf16[48,384]{1,0:T(8,128)(2,1)}, u32[]{:S(2)}) copy-start(bf16[48,384]{1,0:T(8,128)(2,1)} %weight_ref.1) | copy-start | bytes 110596
  309.0 13.6 %copy-start.61 = (f32[1,384]{1,0:T(1,128)S(1)}, f32[1,384]{1,0:T(1,128)}, u32[]{:S(2)}) copy-start(f32[1,384]{1,0:T(1,128)} %broadcast_in_dim.48.skip_ref) | copy-start | bytes 4612
  322.6 28.2 %copy-start.45 = (f32[16,8,384]{2,1,0:T(8,128)S(1)}, f32[16,8,384]{2,1,0:T(8,128)}, u32[]{:S(2)}) copy-start(f32[16,8,384]{2,1,0:T(8,128)} %copy-done.44) | copy-start | bytes 589828
  350.6 3.6 copy-start.60
  350.6 10.9 %copy-start.16 = (bf16[96,8,2,384]{3,1,2,0:T(8,128)(2,1)S(1)}, bf16[96,8,2,384]{3,1,2,0:T(8,128)(2,1)}, u32[]{:S(2)}) copy-start(bf16[96,8,2,384]{3,1,2,0:T(8,128)(2,1)} %copy-done.15) | copy-start | bytes 3538948
  350.6 10.9 %copy-start.43 = (bf16[384,80]{1,0:T(8,128)(2,1)S(1)}, bf16[384,80]{1,0:T(8,128)(2,1)}, u32[]{:S(2)}) copy-start(bf16[384,80]{1,0:T(8,128)(2,1)} %copy.101.select_ref) | copy-start | bytes 184324
  350.6 10.9 %copy-start.46 = (f32[24,384]{1,0:T(8,128)S(1)}, f32[24,384]{1,0:T(8,128)}, u32[]{:S(2)}) copy-start(f32[24,384]{1,0:T(8,128)} %maximum_bitcast_fusion.lead_ref) | copy-start | bytes 110596
  379.6 5.9 %copy-start.72 = (f32[384,768]{1,0:T(8,128)S(1)}, f32[384,768]{1,0:T(8,128)}, u32[]{:S(2)}) copy-start(f32[384,768]{1,0:T(8,128)} %get-tuple-element.63) | copy-start | bytes 3538948
  473.5 6.3 %slice-start = ((f32[1280,768]{1,0:T(8,128)}), f32[768,768]{1,0:T(8,128)S(1)}, s32[]{:S(2)}) async-start(f32[1280,768]{1,0:T(8,128)} %copy-done.65), calls=%async_computation | async-start | bytes 4718592 | tf_op jit(solution)/shard_map/slice | solution.py:1373
  479.8 3.6 slice-start.2
  479.8 4.9 slice-start.3
  479.9 6.1 %copy-start.97 = (f32[768]{0:T(1024)S(1)}, f32[768]{0:T(1024)}, u32[]{:S(2)}) copy-start(f32[768]{0:T(1024)} %get-tuple-element.112) | copy-start | bytes 9220
  479.9 6.7 %copy-start.90 = (f32[768]{0:T(1024)S(1)}, f32[768]{0:T(1024)}, u32[]{:S(2)}) copy-start(f32[768]{0:T(1024)} %get-tuple-element.80) | copy-start | bytes 9220
  487.1 3.9 copy-start.1
  (54 other events, 90.1 us)
